TPU v7x, 32 devices: a whole 2x2x4 slice. The times are simulated.
32 devices in a mesh: dp: 4 (over x, core), ev: 8 (over z, y).
Axes of the slice: x: 2, y: 2, z: 4, core: 2. Of those that a mesh axis runs over, the one named last changes fastest.
Arguments:
- events: bfloat16 [4, 1024, 512], P('dp', 'ev'), may hold values from -25 to 25
- cotangent: bfloat16 [4, 1024, 512], P('dp', 'ev'), may hold values from -6 to 6
- intra_gain: float32 [512], replicated, may hold values from 0.25 to 1.75
- intra_proj: bfloat16 [512, 1536], replicated, may hold values from -27 to 27
- intra_out: bfloat16 [512, 512], replicated, may hold values from -0.25 to 0.25
- cross_norm_gain: float32 [512], replicated, may hold values from 0.25 to 1.75
- cross_input_weight: bfloat16 [512, 1536], replicated, may hold values from -27 to 27
- cross_output_weight: bfloat16 [512, 512], replicated, may hold values from -0.25 to 0.25
- owner_map: int32 [4, 1024], P('dp'), may hold values from 0 to 7, as said below
- block_lists: int32 [4, 8, 2, 2], P('dp', 'ev'), may hold values from 0 to 1
Outputs:
- layer_out: bfloat16 [4, 1024, 512], P('dp', 'ev')
- grad_events: bfloat16 [4, 1024, 512], P('dp', 'ev')
- grad_cross_proj: float32 [512, 1536], P('ev')
- grad_cross_out: float32 [512, 512], P('ev')
Inputs may be any that keep to these rules, and one draw needn't show every extreme that they name: `owner_map`: in each replica no device sends more than 32 rows to one owner.
All inputs are finite; a program needn't handle non-finite values.
Results may differ from a plain program's by a relative error of at most 0.033.
The roundings to bfloat16 on the way count: a program that leaves them out, or rounds other values in their place, can miss the bound.
Values may be sent and summed in bfloat16 or wider, within the bound.
A program may use at most 64 MiB of HBM per device.

v0:
```python
import jax
import jax.numpy as jnp
from jax import lax
from jax.sharding import PartitionSpec as P

HEADS = 8
HEAD_DIM = 64
EVENTS_PER_BLOCK = 128


EPSILON = 1e-05


def layer_norm(values, scale_factors):
    upcast = values.astype(jnp.float32)
    center = upcast - jnp.mean(upcast, axis=-1, keepdims=True)
    spread = jnp.mean(center * center, axis=-1, keepdims=True)
    return center * lax.rsqrt(spread + EPSILON) * scale_factors


def split_heads(matrix, block_groups):
    return matrix.reshape(block_groups, EVENTS_PER_BLOCK, HEADS, HEAD_DIM)


def intra_branch(source, scale_factors, input_weight, output_weight):
    row_total, features = source.shape
    block_groups = row_total // EVENTS_PER_BLOCK
    normed = layer_norm(source, scale_factors).astype(jnp.bfloat16)
    packed_rows = jnp.dot(normed, input_weight, preferred_element_type=jnp.float32).astype(
        jnp.bfloat16
    )
    queries = split_heads(packed_rows[:, :features], block_groups).astype(jnp.float32)
    key_rows = split_heads(packed_rows[:, features : 2 * features], block_groups).astype(
        jnp.float32
    )
    value_rows = split_heads(packed_rows[:, 2 * features :], block_groups).astype(jnp.float32)
    scores = jnp.einsum("bqhd,bkhd->bhqk", queries, key_rows) * HEAD_DIM ** (-0.5)
    highest = jnp.max(scores, axis=-1, keepdims=True)
    weights = jnp.exp(scores - highest)
    attention = (weights / jnp.sum(weights, axis=-1, keepdims=True)).astype(jnp.bfloat16)
    merged_rows = jnp.einsum("bhqk,bkhd->bqhd", attention.astype(jnp.float32), value_rows)
    merged_rows = merged_rows.astype(jnp.bfloat16).reshape(row_total, features)
    branch = jnp.dot(merged_rows, output_weight, preferred_element_type=jnp.float32)
    return (source.astype(jnp.float32) + branch).astype(jnp.bfloat16)


def cross_account_inner(packed_rows, row_presence, block_listing):
    row_total, three_wide = packed_rows.shape
    features = three_wide // 3
    block_groups = row_total // EVENTS_PER_BLOCK
    selected_rows = jnp.concatenate(
        [jnp.arange(block_groups, dtype=jnp.int32)[:, None], block_listing], axis=1
    )
    queries = split_heads(packed_rows[:, :features].astype(jnp.float32), block_groups)
    key_rows = split_heads(
        packed_rows[:, features : 2 * features].astype(jnp.float32), block_groups
    )[selected_rows]
    key_rows = key_rows.reshape(block_groups, -1, HEADS, HEAD_DIM)
    value_rows = split_heads(packed_rows[:, 2 * features :].astype(jnp.float32), block_groups)[
        selected_rows
    ]
    value_rows = value_rows.reshape(block_groups, -1, HEADS, HEAD_DIM)
    key_present = row_presence.reshape(block_groups, EVENTS_PER_BLOCK)[selected_rows].reshape(
        block_groups, -1
    )
    key_total = key_present.shape[1]
    itself = (
        jnp.arange(key_total, dtype=jnp.int32)[None, :]
        == jnp.arange(EVENTS_PER_BLOCK, dtype=jnp.int32)[:, None]
    )
    allowed = key_present[:, None, None, :] | itself[None, None, :, :]
    scores = jnp.einsum("bqhd,bkhd->bhqk", queries, key_rows) * HEAD_DIM ** (-0.5)
    scores = jnp.where(allowed, scores, -1e30)
    highest = jnp.max(scores, axis=-1, keepdims=True)
    weights = jnp.where(allowed, jnp.exp(scores - highest), 0.0)
    attention = (weights / jnp.sum(weights, axis=-1, keepdims=True)).astype(jnp.bfloat16)
    merged_rows = jnp.einsum("bhqk,bkhd->bqhd", attention.astype(jnp.float32), value_rows)
    return merged_rows.astype(jnp.bfloat16).reshape(row_total, features)


def owner_transfer(
    landed_rows,
    landed_cotangent,
    row_presence,
    block_listing,
    scale_factors,
    input_weight,
    output_weight,
):
    normed, norm_pull = jax.vjp(
        lambda input_operand: layer_norm(input_operand, scale_factors), landed_rows
    )
    normed_half = normed.astype(jnp.bfloat16)
    packed_rows = jnp.dot(normed_half, input_weight, preferred_element_type=jnp.float32).astype(
        jnp.bfloat16
    )
    merged_rows, central_gather = jax.vjp(
        lambda input_operand: cross_account_inner(input_operand, row_presence, block_listing),
        packed_rows,
    )
    result = jnp.dot(merged_rows, output_weight, preferred_element_type=jnp.float32).astype(
        jnp.bfloat16
    )
    back_mixed = lax.dot_general(
        landed_cotangent,
        output_weight,
        (((1,), (1,)), ((), ())),
        preferred_element_type=jnp.float32,
    ).astype(jnp.bfloat16)
    back_packed = central_gather(back_mixed)[0]
    back_normed = lax.dot_general(
        back_packed, input_weight, (((1,), (1,)), ((), ())), preferred_element_type=jnp.float32
    )
    back_rows = norm_pull(back_normed)[0]
    return (result, back_rows, normed_half, back_packed, merged_rows)


def contract(left_part, right_part):
    return lax.dot_general(
        left_part, right_part, (((0,), (0,)), ((), ())), preferred_element_type=jnp.float32
    )


def on_device(
    events,
    cotangent,
    intra_gain,
    intra_proj,
    intra_out,
    cross_norm_gain,
    cross_input_weight,
    cross_output_weight,
    owner_map,
    block_lists,
):
    rows_here = events[0]
    upstream = cotangent[0]
    local_rows, features = rows_here.shape
    owners = lax.axis_size("ev")
    replicas = lax.axis_size("dp")
    own_index = lax.axis_index("ev")
    row_capacity = 2 * local_rows // owners
    buffer_rows = owners * row_capacity
    hidden, intra_pull = jax.vjp(
        lambda input_operand: intra_branch(input_operand, intra_gain, intra_proj, intra_out),
        rows_here,
    )
    targets = owner_map[0]
    onehot = (targets[:, None] == jnp.arange(owners, dtype=jnp.int32)[None, :]).astype(jnp.int32)
    row_counts = jnp.sum(onehot.reshape(owners, local_rows, owners), axis=1)
    inbound_rows = lax.dynamic_index_in_dim(row_counts, own_index, axis=1, keepdims=False)
    own_onehot = lax.dynamic_slice_in_dim(onehot, own_index * local_rows, local_rows, 0)
    before = jnp.cumsum(own_onehot, axis=0) - own_onehot
    slot_ids = jnp.sum(before * own_onehot, axis=1)
    own_dest = lax.dynamic_slice_in_dim(targets, own_index * local_rows, local_rows, 0)
    position = own_dest * row_capacity + slot_ids
    outgoing = jnp.zeros((buffer_rows, features), jnp.bfloat16).at[position].set(hidden)
    pending = jnp.zeros((buffer_rows, features), jnp.bfloat16).at[position].set(upstream)
    landed_rows = lax.all_to_all(outgoing, "ev", split_axis=0, concat_axis=0, tiled=True)
    landed_cotangent = lax.all_to_all(pending, "ev", split_axis=0, concat_axis=0, tiled=True)
    row_presence = (
        jnp.arange(row_capacity, dtype=jnp.int32)[None, :] < inbound_rows[:, None]
    ).reshape(buffer_rows)
    block_listing = block_lists[0, 0]
    result, back_rows, normed_half, back_packed, merged_rows = owner_transfer(
        landed_rows,
        landed_cotangent,
        row_presence,
        block_listing,
        cross_norm_gain,
        cross_input_weight,
        cross_output_weight,
    )
    returned, sent_back = (
        lax.all_to_all(result, "ev", split_axis=0, concat_axis=0, tiled=True),
        lax.all_to_all(back_rows, "ev", split_axis=0, concat_axis=0, tiled=True),
    )
    layer_out = (hidden.astype(jnp.float32) + returned[position].astype(jnp.float32)).astype(
        jnp.bfloat16
    )
    grad_hidden = (upstream.astype(jnp.float32) + sent_back[position].astype(jnp.float32)).astype(
        jnp.bfloat16
    )
    grad_rows = intra_pull(grad_hidden)[0]
    factor = (replicas * owners * local_rows) ** (-0.5)
    partial_sum = jnp.concatenate(
        [contract(normed_half, back_packed), contract(merged_rows, landed_cotangent)], axis=1
    )
    summed = lax.psum(partial_sum.astype(jnp.bfloat16), "dp")
    portion = lax.psum_scatter(summed, "ev", scatter_dimension=0, tiled=True).astype(jnp.float32)
    portion = portion * factor
    return (
        layer_out[None],
        grad_rows[None],
        portion[:, : 3 * features],
        portion[:, 3 * features :],
    )


def solution(mesh):
    return jax.shard_map(
        on_device,
        mesh=mesh,
        in_specs=(
            P("dp", "ev", None),
            P("dp", "ev", None),
            P(),
            P(),
            P(),
            P(),
            P(),
            P(),
            P("dp", None),
            P("dp", "ev", None, None),
        ),
        out_specs=(P("dp", "ev", None), P("dp", "ev", None), P("ev", None), P("ev", None)),
        check_vma=False,
    )
```

profile of v0, /device:TPU:0, one launch (start us, length us, event | category | flops | bytes accessed | tf_op | source)
XLA Modules:
  0.0 241.6 jit_solution(8611395975291636877)
XLA Ops:
  13.0 2.0 convolution_convert_fusion.2
  17.5 1.9 scatter_custom_fusion
  19.4 7.3 %all-to-all-start = ((bf16[8,32,512]{2,1,0:T(8,128)(2,1)}), bf16[8,32,512]{2,1,0:T(8,128)(2,1)S(1)}, u32[]{:S(2)}, u32[]{:S(2)}) async-start(bf16[8,32,512]{2,1,0:T(8,128)(2,1)} %bitcast.11), calls=%async_computation | async-start | bytes 524288 | tf_op jit(solution)/shard_map/all_to_all | solution.py:159
  28.9 1.9 scatter_custom_fusion.1
  31.4 4.1 %all-to-all-done = bf16[8,32,512]{2,1,0:T(8,128)(2,1)S(1)} async-done(((bf16[8,32,512]{2,1,0:T(8,128)(2,1)}), bf16[8,32,512]{2,1,0:T(8,128)(2,1)S(1)}, u32[]{:S(2)}, u32[]{:S(2)}) %all-to-all-start) | async-done | bytes 262176 | tf_op jit(solution)/shard_map/all_to_all | solution.py:159
  35.6 4.2 %all-to-all-start.2 = ((bf16[8,32,512]{2,1,0:T(8,128)(2,1)}), bf16[8,32,512]{2,1,0:T(8,128)(2,1)}, u32[]{:S(2)}, u32[]{:S(2)}) async-start(bf16[8,32,512]{2,1,0:T(8,128)(2,1)} %bitcast.20), calls=%async_computation.2 | async-start | bytes 524288 | tf_op jit(solution)/shard_map/all_to_all | solution.py:160
  50.1 2.9 %reshape.397 = bf16[2,384,8,64]{1,0,3,2:T(2,128)(2,1)} reshape(bf16[6,128,8,64]{1,0,3,2:T(8,128)(2,1)} %copy.134) | data formatting | bytes 1572864 | tf_op jit(solution)/shard_map/jvp()/reshape | solution.py:58
  56.0 2.2 reshape.394
  58.2 2.3 fusion.92
  60.5 1.7 copy-done.1
  63.4 2.2 convolution_convert_fusion.6
  65.6 1.8 copy.139
  67.4 1.7 reshape.399
  69.1 3.6 %fusion.4 = (f32[2,8,128]{2,1,0:T(8,128)S(1)}, bf16[2,8,128,384]{3,2,1,0:T(8,128)(2,1)S(1)}) fusion(f32[2,8,128,384]{3,2,1,0:T(8,128)} %copy-done.1, f32[2,8,128]{2,1,0:T(8,128)S(1)} %multiply_divide_fusion, f32[2,8,128]{2,1,0:T(8,128)S(1)} %get-tuple-element.25, pred[2,128,384]{2,1,0:T(8,128)(4,1)S(1)} %copy-done.11, ...), kind=kOutput, calls=%fused_computation.15 | convolution fusion | flops 106166272 | bytes 5890048 | tf_op jit(solution)/shard_map/transpose(jvp(bhqk,bkhd->bqhd))/dot_general | solution.py:77
  72.7 3.0 %fusion.86 = (f32[2,8,128]{2,1,0:T(8,128)S(1)}, bf16[2,8,128,384]{3,2,1,0:T(8,128)(2,1)S(1)}, f32[2,8,128]{2,1,0:T(8,128)S(1)}, pred[2,8,128,384]{3,2,1,0:T(32,128)(4,1)S(1)}) fusion(f32[2,8,128,384]{3,2,1,0:T(8,128)S(1)} %copy-done.2, f32[2,8,128]{2,1,0:T(8,128)S(1)} %get-tuple-element.25, f32[2,8,128]{2,1,0:T(8,128)S(1)} %neg.25, ...), kind=kLoop, calls=%fused_computation.170 | loop fusion | flops 10219520 | bytes 7217152 | tf_op jit(solution)/shard_map/transpose(jvp())/reduce_sum | solution.py:75
  75.8 3.3 %fusion.21 = bf16[2,128,8,64]{1,3,2,0:T(8,128)(2,1)} fusion(pred[2,8,128,384]{3,2,1,0:T(32,128)(4,1)S(1)} %get-tuple-element.15, f32[2,8,128]{2,1,0:T(8,128)S(1)} %negate_divide_fusion, pred[2,128,384]{2,1,0:T(8,128)(4,1)S(1)} %copy-done.11, bf16[2,384,8,64]{1,0,3,2:T(2,128)(2,1)S(1)} %copy-done.4, bf16[2,8,128,384]{3,2,1,0:T(8,128)(2,1)S(1)} %get-tuple-element.28, ...), kind=kOutput, calls=%fused_computation.51 | convolution fusion | flops 108658688 | bytes 6684672 | tf_op jit(solution)/shard_map/transpose(jvp(bqhd,bkhd->bhqk))/dot_general | solution.py:72
  79.1 3.7 %fusion.17 = f32[2,384,8,64]{1,3,2,0:T(8,128)} fusion(bf16[2,128,8,64]{1,3,2,0:T(8,128)(2,1)S(1)} %copy-done.21, pred[2,8,128,384]{3,2,1,0:T(32,128)(4,1)S(1)} %get-tuple-element.15, f32[2,8,128]{2,1,0:T(8,128)S(1)} %negate_divide_fusion, pred[2,128,384]{2,1,0:T(8,128)(4,1)S(1)} %copy-done.11, bf16[2,8,128,384]{3,2,1,0:T(8,128)(2,1)S(1)} %get-tuple-element.28, ...), kind=kOutput, calls=%fused_computation.39 | convolution fusion | flops 108527616 | bytes 7471104 | tf_op jit(solution)/shard_map/transpose(jvp(bqhd,bkhd->bhqk))/dot_general | solution.py:72
  86.5 2.1 convolution_convert_fusion.4
  88.5 5.7 %all-to-all-start.1 = ((bf16[8,32,512]{2,1,0:T(8,128)(2,1)}), bf16[8,32,512]{2,1,0:T(8,128)(2,1)S(1)}, u32[]{:S(2)}, u32[]{:S(2)}) async-start(bf16[8,32,512]{2,1,0:T(8,128)(2,1)} %bitcast.16), calls=%async_computation.1 | async-start | bytes 524288 | tf_op jit(solution)/shard_map/all_to_all | solution.py:175
  95.3 3.8 %copy.147 = f32[2,384,8,64]{1,0,3,2:T(2,128)} copy(f32[2,384,8,64]{1,3,2,0:T(8,128)} %fusion.17) | data formatting | bytes 3145728 | tf_op jit(solution)/shard_map/transpose(jvp(bqhd,bkhd->bhqk))/transpose | solution.py:72
  99.1 3.5 %reshape.476 = f32[6,128,8,64]{1,0,3,2:T(8,128)} reshape(f32[2,384,8,64]{1,0,3,2:T(2,128)} %copy.147) | data formatting | bytes 3145728 | tf_op jit(solution)/shard_map/transpose(jvp())/reshape | solution.py:58
  102.6 3.1 %copy.148 = f32[6,128,8,64]{1,3,2,0:T(8,128)} copy(f32[6,128,8,64]{1,0,3,2:T(8,128)} %reshape.476) | data formatting | bytes 3145728 | tf_op jit(solution)/shard_map/transpose(jvp())/reshape | solution.py:58
  105.7 2.8 %scatter_fusion.1 = f32[2,128,8,64]{1,3,2,0:T(8,128)S(1)} fusion(f32[2,128,8,64]{1,3,2,0:T(8,128)S(1)} %broadcast.222.clone, s32[6]{0:T(128)S(1)} %reshape.410, f32[6,128,8,64]{1,3,2,0:T(8,128)} %copy.148), kind=kCustom, calls=%fused_computation.8 | custom fusion | flops 393216 | bytes 4718616 | tf_op jit(solution)/shard_map/transpose(jvp())/scatter-add | solution.py:55
  109.5 3.8 %copy.141 = f32[2,384,8,64]{1,0,3,2:T(2,128)} copy(f32[2,384,8,64]{1,3,2,0:T(8,128)} %convolution_bitcast_fusion) | data formatting | bytes 3145728 | tf_op jit(solution)/shard_map/transpose(jvp(bhqk,bkhd->bqhd))/transpose | solution.py:77
  113.3 3.5 %reshape.468 = f32[6,128,8,64]{1,0,3,2:T(8,128)} reshape(f32[2,384,8,64]{1,0,3,2:T(2,128)} %copy.141) | data formatting | bytes 3145728 | tf_op jit(solution)/shard_map/transpose(jvp())/reshape | solution.py:62
  116.8 3.0 %copy.142 = f32[6,128,8,64]{1,3,2,0:T(8,128)} copy(f32[6,128,8,64]{1,0,3,2:T(8,128)} %reshape.468) | data formatting | bytes 3145728 | tf_op jit(solution)/shard_map/transpose(jvp())/reshape | solution.py:62
  119.9 2.8 %scatter_fusion = f32[2,128,8,64]{1,3,2,0:T(8,128)S(1)} fusion(f32[2,128,8,64]{1,3,2,0:T(8,128)S(1)} %broadcast.222.clone.1, s32[6]{0:T(128)S(1)} %reshape.410, f32[6,128,8,64]{1,3,2,0:T(8,128)} %copy.142), kind=kCustom, calls=%fused_computation.7 | custom fusion | flops 393216 | bytes 4718616 | tf_op jit(solution)/shard_map/transpose(jvp())/scatter-add | solution.py:59
  125.6 1.6 pad_maximum_fusion
  129.8 6.0 %all-to-all-start.3 = ((bf16[8,32,512]{2,1,0:T(8,128)(2,1)}), bf16[8,32,512]{2,1,0:T(8,128)(2,1)S(1)}, u32[]{:S(2)}, u32[]{:S(2)}) async-start(bf16[8,32,512]{2,1,0:T(8,128)(2,1)} %bitcast.26), calls=%async_computation.3 | async-start | bytes 524288 | tf_op jit(solution)/shard_map/all_to_all | solution.py:176
  137.9 10.7 %all-to-all-done.3 = bf16[8,32,512]{2,1,0:T(8,128)(2,1)S(1)} async-done(((bf16[8,32,512]{2,1,0:T(8,128)(2,1)}), bf16[8,32,512]{2,1,0:T(8,128)(2,1)S(1)}, u32[]{:S(2)}, u32[]{:S(2)}) %all-to-all-start.3) | async-done | bytes 262176 | tf_op jit(solution)/shard_map/all_to_all | solution.py:176
  156.8 42.2 %reduce-scatter.2.cloned.1.call-done = bf16[64,2048]{1,0:T(8,128)(2,1)} async-done(((bf16[512,2048]{1,0:T(8,128)(2,1)}), bf16[64,2048]{1,0:T(8,128)(2,1)}) %reduce-scatter.2.cloned.1.call-update) | async-done | bytes 262160 | tf_op jit(solution)/shard_map/reduce_scatter | solution.py:190
  199.8 32.6 %all-reduce.8.cloned.1.call-done = bf16[64,2048]{1,0:T(8,128)(2,1)} async-done(((bf16[64,2048]{1,0:T(8,128)(2,1)}), bf16[64,2048]{1,0:T(8,128)(2,1)}) %all-reduce.8.cloned.1.call-update) | async-done | bytes 262160 | tf_op jit(solution)/shard_map/psum | solution.py:189
  (198 shorter events, 50.0 us)
Async XLA Ops:
  7.2 35.1 %copy-start = (bf16[512,1536]{1,0:T(8,128)(2,1)S(1)}, bf16[512,1536]{1,0:T(8,128)(2,1)}, u32[]{:S(2)}) copy-start(bf16[512,1536]{1,0:T(8,128)(2,1)} %param.16) | copy-start | bytes 4718596
  13.0 4.2 %copy-start.3 = (bf16[1,128,512]{2,1,0:T(8,128)(2,1)S(1)}, bf16[1,128,512]{2,1,0:T(8,128)(2,1)}, u32[]{:S(2)}) copy-start(bf16[1,128,512]{2,1,0:T(8,128)(2,1)} %param.10) | copy-start | bytes 393220
  13.0 4.2 %copy-start.9 = (bf16[512,512]{1,0:T(8,128)(2,1)S(1)}, bf16[512,512]{1,0:T(8,128)(2,1)}, u32[]{:S(2)}) copy-start(bf16[512,512]{1,0:T(8,128)(2,1)} %param.14) | copy-start | bytes 1572868
  15.0 11.7 %copy-start.42 = (s32[1,1024]{1,0:T(1,128)S(1)}, s32[1,1024]{1,0:T(1,128)}, u32[]{:S(2)}) copy-start(s32[1,1024]{1,0:T(1,128)} %param.18) | copy-start | bytes 12292
  15.0 13.8 %copy-start.14 = (bf16[1,128,512]{2,1,0:T(8,128)(2,1)S(1)}, bf16[1,128,512]{2,1,0:T(8,128)(2,1)}, u32[]{:S(2)}) copy-start(bf16[1,128,512]{2,1,0:T(8,128)(2,1)} %param.11) | copy-start | bytes 393220
  15.2 24.8 %copy-start.20 = (bf16[128,512]{0,1:T(8,128)(2,1)}, bf16[128,512]{0,1:T(8,128)(2,1)S(1)}, u32[]{:S(2)}) copy-start(bf16[128,512]{0,1:T(8,128)(2,1)S(1)} %copy.124) | copy-start | bytes 393220
  17.0 23.3 %copy-start.7 = (bf16[8,128,128]{1,2,0:T(8,128)(2,1)}, bf16[8,128,128]{1,2,0:T(8,128)(2,1)S(1)}, u32[]{:S(2)}) copy-start(bf16[8,128,128]{1,2,0:T(8,128)(2,1)S(1)} %get-tuple-element.19) | copy-start | bytes 786436
  19.4 16.2 %all-to-all-start = ((bf16[8,32,512]{2,1,0:T(8,128)(2,1)}), bf16[8,32,512]{2,1,0:T(8,128)(2,1)S(1)}, u32[]{:S(2)}, u32[]{:S(2)}) async-start(bf16[8,32,512]{2,1,0:T(8,128)(2,1)} %bitcast.11), calls=%async_computation | async-start | bytes 524288 | tf_op jit(solution)/shard_map/all_to_all | solution.py:159
  35.6 27.8 %all-to-all-start.2 = ((bf16[8,32,512]{2,1,0:T(8,128)(2,1)}), bf16[8,32,512]{2,1,0:T(8,128)(2,1)}, u32[]{:S(2)}, u32[]{:S(2)}) async-start(bf16[8,32,512]{2,1,0:T(8,128)(2,1)} %bitcast.20), calls=%async_computation.2 | async-start | bytes 524288 | tf_op jit(solution)/shard_map/all_to_all | solution.py:160
  42.3 5.1 %copy-start.22 = (bf16[256,512]{1,0:T(8,128)(2,1)}, bf16[256,512]{1,0:T(8,128)(2,1)S(1)}, u32[]{:S(2)}) copy-start(bf16[256,512]{1,0:T(8,128)(2,1)S(1)} %multiply_convert_fusion) | copy-start | bytes 786436
  48.5 4.4 %copy-start.24 = (bf16[256,512]{1,0:T(8,128)(2,1)S(1)}, bf16[256,512]{1,0:T(8,128)(2,1)}, u32[]{:S(2)}) copy-start(bf16[256,512]{1,0:T(8,128)(2,1)} %get-tuple-element.16) | copy-start | bytes 786436
  56.0 6.2 %copy-start.11 = (pred[2,128,384]{2,1,0:T(8,128)(4,1)S(1)}, pred[2,128,384]{2,1,0:T(8,128)(4,1)}, u32[]{:S(2)}) copy-start(pred[2,128,384]{2,1,0:T(8,128)(4,1)} %broadcast_or_fusion) | copy-start | bytes 294916
  58.2 10.9 %copy-start.5 = (bf16[2,384,8,64]{1,0,3,2:T(2,128)(2,1)}, bf16[2,384,8,64]{1,0,3,2:T(2,128)(2,1)S(1)}, u32[]{:S(2)}) copy-start(bf16[2,384,8,64]{1,0,3,2:T(2,128)(2,1)S(1)} %reshape.394) | copy-start | bytes 2359300
  69.1 3.6 %copy-start.2 = (f32[2,8,128,384]{3,2,1,0:T(8,128)S(1)}, f32[2,8,128,384]{3,2,1,0:T(8,128)}, u32[]{:S(2)}) copy-start(f32[2,8,128,384]{3,2,1,0:T(8,128)} %copy-done.1) | copy-start | bytes 9437188
  79.1 3.7 %copy-start.6 = (bf16[2,384,8,64]{1,0,3,2:T(2,128)(2,1)S(1)}, bf16[2,384,8,64]{1,0,3,2:T(2,128)(2,1)}, u32[]{:S(2)}) copy-start(bf16[2,384,8,64]{1,0,3,2:T(2,128)(2,1)} %copy-done.5) | copy-start | bytes 2359300
  79.1 4.5 %copy-start.25 = (bf16[2,128,8,64]{1,0,3,2:T(2,128)(2,1)S(1)}, bf16[2,128,8,64]{1,0,3,2:T(2,128)(2,1)}, u32[]{:S(2)}) copy-start(bf16[2,128,8,64]{1,0,3,2:T(2,128)(2,1)} %reshape.399) | copy-start | bytes 786436
  83.6 10.7 %copy-start.30 = (bf16[2,128,8,64]{1,3,2,0:T(8,128)(2,1)S(1)}, bf16[2,128,8,64]{1,3,2,0:T(8,128)(2,1)}, u32[]{:S(2)}) copy-start(bf16[2,128,8,64]{1,3,2,0:T(8,128)(2,1)} %fusion.21) | copy-start | bytes 786436
  88.5 41.2 %all-to-all-start.1 = ((bf16[8,32,512]{2,1,0:T(8,128)(2,1)}), bf16[8,32,512]{2,1,0:T(8,128)(2,1)S(1)}, u32[]{:S(2)}, u32[]{:S(2)}) async-start(bf16[8,32,512]{2,1,0:T(8,128)(2,1)} %bitcast.16), calls=%async_computation.1 | async-start | bytes 524288 | tf_op jit(solution)/shard_map/all_to_all | solution.py:175
  94.3 104.8 %reduce-scatter.2.cloned.1.call-start = ((), (), s32[]{:S(2)}) async-start(), calls=%async_computation.5 | async-start | bytes 2359296 | tf_op jit(solution)/shard_map/reduce_scatter | solution.py:190
  119.9 5.0 %copy-start.23 = (bf16[256,512]{1,0:T(8,128)(2,1)S(1)}, bf16[256,512]{1,0:T(8,128)(2,1)}, u32[]{:S(2)}) copy-start(bf16[256,512]{1,0:T(8,128)(2,1)} %copy-done.22) | copy-start | bytes 786436
  128.6 20.8 %copy-start.15 = (bf16[1,128,512]{2,1,0:T(8,128)(2,1)S(1)}, bf16[1,128,512]{2,1,0:T(8,128)(2,1)}, u32[]{:S(2)}) copy-start(bf16[1,128,512]{2,1,0:T(8,128)(2,1)} %param.11) | copy-start | bytes 393220
  129.8 18.8 %all-to-all-start.3 = ((bf16[8,32,512]{2,1,0:T(8,128)(2,1)}), bf16[8,32,512]{2,1,0:T(8,128)(2,1)S(1)}, u32[]{:S(2)}, u32[]{:S(2)}) async-start(bf16[8,32,512]{2,1,0:T(8,128)(2,1)} %bitcast.26), calls=%async_computation.3 | async-start | bytes 524288 | tf_op jit(solution)/shard_map/all_to_all | solution.py:176
  135.7 96.6 %all-reduce.8.cloned.1.call-start = ((), (), s32[]{:S(2)}) async-start(), calls=%async_computation.6 | async-start | bytes 524288 | tf_op jit(solution)/shard_map/psum | solution.py:189
  136.4 16.1 %copy-start.8 = (bf16[8,128,128]{1,2,0:T(8,128)(2,1)S(1)}, bf16[8,128,128]{1,2,0:T(8,128)(2,1)}, u32[]{:S(2)}) copy-start(bf16[8,128,128]{1,2,0:T(8,128)(2,1)} %copy-done.7) | copy-start | bytes 786436
  137.9 15.0 %copy-start.13 = (pred[8,128,128]{1,2,0:T(32,128)(4,1)S(1)}, pred[8,128,128]{1,2,0:T(32,128)(4,1)}, u32[]{:S(2)}) copy-start(pred[8,128,128]{1,2,0:T(32,128)(4,1)} %get-tuple-element.7) | copy-start | bytes 393220
  149.5 4.6 %copy-start.18 = (bf16[128,512]{0,1:T(8,128)(2,1)S(1)}, bf16[128,512]{0,1:T(8,128)(2,1)}, u32[]{:S(2)}) copy-start(bf16[128,512]{0,1:T(8,128)(2,1)} %copy-done.17) | copy-start | bytes 393220
  152.3 3.4 %copy-start.46 = (f32[128]{0:T(128)S(1)}, f32[128]{0:T(128)}, u32[]{:S(2)}) copy-start(f32[128]{0:T(128)} %copy-done.45) | copy-start | bytes 1540
  152.3 3.5 %copy-start.41 = (f32[128]{0:T(128)S(1)}, f32[128]{0:T(128)}, u32[]{:S(2)}) copy-start(f32[128]{0:T(128)} %copy-done.40) | copy-start | bytes 1540
  152.4 3.5 %copy-start.44 = (f32[128]{0:T(128)S(1)}, f32[128]{0:T(128)}, u32[]{:S(2)}) copy-start(f32[128]{0:T(128)} %copy-done.43) | copy-start | bytes 1540
  152.5 3.5 %copy-start.16 = (bf16[1,128,512]{2,1,0:T(8,128)(2,1)S(1)}, bf16[1,128,512]{2,1,0:T(8,128)(2,1)}, u32[]{:S(2)}) copy-start(bf16[1,128,512]{2,1,0:T(8,128)(2,1)} %param.11) | copy-start | bytes 393220
  152.8 46.3 %copy-start.27 = (bf16[128,512]{1,0:T(8,128)(2,1)S(1)}, bf16[128,512]{1,0:T(8,128)(2,1)}, u32[]{:S(2)}) copy-start(bf16[128,512]{1,0:T(8,128)(2,1)} %copy-done.26) | copy-start | bytes 393220
  152.8 46.3 %copy-start.28 = (bf16[128,512]{1,0:T(8,128)(2,1)S(1)}, bf16[128,512]{1,0:T(8,128)(2,1)}, u32[]{:S(2)}) copy-start(bf16[128,512]{1,0:T(8,128)(2,1)} %gather_fusion.3) | copy-start | bytes 393220
  (21 other events, 32.1 us)
Sparse Core Ops, SparseCore 0:
  127.3 71.6 reduce-scatter.1
  201.4 30.9 all-reduce.7
where the time goes:
time: 243 us; the launch traced here: 242 us
  waiting for transfers between devices  89.6 us (37%)
  local copies, waits for them, and re-layouts  58.5 us (24%)
  matrix products  31.7 us (13%)
  other arithmetic  23.6 us (10%)
  starting transfers between devices  23.3 us (10%)
  between operations  15 us (6%)
    reduce_scatter x1, waiting for transfers between devices, on_device(): lax.psum_scatter(summed, 'ev', scatter_dimension=0, tiled=True)  42.2 us
    psum x1, waiting for transfers between devices, on_device(): summed = lax.psum(partial_sum.astype(jnp.bfloat16), 'dp')  32.6 us
    all_to_all x1, waiting for transfers between devices, on_device(): lax.all_to_all(back_rows, 'ev', split_axis=0, concat_axis=0, tiled=True)  10.7 us
    reshape x3, local copies, waits for them, and re-layouts, cross_account_inner(): key_rows = key_rows.reshape(block_groups, -1, HEADS, HEAD_DIM)  9.42 us
    dot_general x3, matrix products, cross_account_inner(): jnp.einsum('bqhd,bkhd->bhqk', queries, key_rows) * HEAD_DIM ** (-0.5)  9.3 us
    reshape x3, local copies, waits for them, and re-layouts, cross_account_inner(): value_rows = value_rows.reshape(block_groups, -1, HEADS, HEAD_DIM)  8.71 us
    all_to_all x1, starting transfers between devices, on_device(): lax.all_to_all(outgoing, 'ev', split_axis=0, concat_axis=0, tiled=True)  7.28 us
    dot_general x3, matrix products, cross_account_inner(): jnp.einsum('bhqk,bkhd->bqhd', attention.astype(jnp.float32), value_rows)  5.97 us
  transfers between devices with their start and end apart: 6, of which 4 were waited for; matrix products, arithmetic and copies ran while one was open for 29% of the time, Pallas kernels for 0%

commit v1 on v0

v1 whole, which is shorter than its diff:
```python
import functools

import jax
import jax.numpy as jnp
from jax import lax
from jax.experimental import pallas as pl
from jax.experimental.pallas import tpu as pltpu
from jax.sharding import PartitionSpec as P

HEAD_DIM = 64
BLOCK = 128
SCALE = HEAD_DIM ** (-0.5)
EPSILON = 1e-05
F32 = jnp.float32
BF16 = jnp.bfloat16
VMEM_LIMIT = 50 * 1024 * 1024
MESH = pl.DeviceIdType.MESH


def dot(a, b):
    return lax.dot_general(a, b, (((1,), (0,)), ((), ())), preferred_element_type=F32)


def dot_bt(a, b):
    return lax.dot_general(a, b, (((1,), (1,)), ((), ())), preferred_element_type=F32)


def dot_at(a, b):
    return lax.dot_general(a, b, (((0,), (0,)), ((), ())), preferred_element_type=F32)


def iota(shape, dim):
    return lax.broadcasted_iota(jnp.int32, shape, dim)


def norm_stats(x):
    center = x - jnp.mean(x, axis=-1, keepdims=True)
    rstd = lax.rsqrt(jnp.mean(center * center, axis=-1, keepdims=True) + EPSILON)
    return center, rstd


def norm_back(x, gain, dy):
    center, rstd = norm_stats(x)
    xhat = center * rstd
    g = dy * gain
    return rstd * (
        g
        - jnp.mean(g, axis=-1, keepdims=True)
        - xhat * jnp.mean(g * xhat, axis=-1, keepdims=True)
    )


def lane_masks(dtype):
    lane = iota((1, 2 * HEAD_DIM), 1)
    low = jnp.where(lane < HEAD_DIM, 1.0, 0.0).astype(F32)
    return low.astype(dtype), (1.0 - low).astype(dtype)


def two_heads(x):
    low, high = lane_masks(BF16)
    return jnp.concatenate([x * low, x * high], axis=0)


def join_heads(x):
    low, high = lane_masks(F32)
    half = x.shape[0] // 2
    return x[:half] * low + x[half:] * high


def owner_rows(owner_ref, owners):
    return jnp.concatenate(
        [owner_ref[:, s * BLOCK : (s + 1) * BLOCK] for s in range(owners)], axis=0
    )


def placement(owner_ref, owners, cap, me):
    table = owner_rows(owner_ref, owners)
    own = jnp.sum(jnp.where(iota(table.shape, 0) == me, table, 0), axis=0, keepdims=True)
    onehot = jnp.where(iota((owners, BLOCK), 0) == own, 1.0, 0.0).astype(F32)
    earlier = jnp.where(iota((BLOCK, BLOCK), 0) < iota((BLOCK, BLOCK), 1), 1.0, 0.0)
    before = dot(onehot.astype(BF16), earlier.astype(BF16))
    slot = jnp.sum(before * onehot, axis=0, keepdims=True).astype(jnp.int32)
    position = own * (2 * cap) + slot
    both = jnp.concatenate([position, position + cap], axis=1)
    hit = iota((owners * 2 * cap, 2 * BLOCK), 0) == both
    return jnp.where(hit, 1.0, 0.0).astype(BF16)


def intra_forward(owners, cap, x_ref, ct_ref, gain_ref, win_ref, wout_ref, om_ref,
                  hid_ref, send_ref, packed_ref, probs_ref):
    me = lax.axis_index("ev")
    d = x_ref.shape[-1]
    x = x_ref[0].astype(F32)
    center, rstd = norm_stats(x)
    normed = (center * rstd * gain_ref[...]).astype(BF16)
    packed = dot(normed, win_ref[...]).astype(BF16)
    packed_ref[...] = packed
    mixed = []
    for t in range(d // BLOCK):
        q = packed[:, t * BLOCK : (t + 1) * BLOCK]
        k = packed[:, d + t * BLOCK : d + (t + 1) * BLOCK]
        v = packed[:, 2 * d + t * BLOCK : 2 * d + (t + 1) * BLOCK]
        s = dot_bt(two_heads(q), k) * SCALE
        w = jnp.exp(s - jnp.max(s, axis=-1, keepdims=True))
        p = w / jnp.sum(w, axis=-1, keepdims=True)
        probs_ref[t] = p
        mixed.append(join_heads(dot(p.astype(BF16), v)).astype(BF16))
    branch = dot(jnp.concatenate(mixed, axis=1), wout_ref[...])
    hidden = (x + branch).astype(BF16)
    hid_ref[...] = hidden
    place = placement(om_ref, owners, cap, me)
    stacked = jnp.concatenate([hidden, ct_ref[0]], axis=0)
    rows = dot(place, stacked).astype(BF16)
    for s in range(owners):
        send_ref[s] = rows[s * 2 * cap : (s + 1) * 2 * cap]


def greet(peers):
    barrier = pltpu.get_barrier_semaphore()
    for peer in peers:
        pl.semaphore_signal(barrier, inc=1, device_id=peer, device_id_type=MESH)
    pl.semaphore_wait(barrier, len(peers))


def exchange(owners, me, send, recv, ssem, rsem):
    copies = []
    for o in range(1, owners):
        to = lax.rem(me + o, owners)
        copies.append(
            pltpu.make_async_remote_copy(
                src_ref=send.at[to], dst_ref=recv.at[me],
                send_sem=ssem.at[o], recv_sem=rsem.at[o],
                device_id=(lax.axis_index("dp"), to), device_id_type=MESH,
            )
        )
    return copies


def exchange_kernel(owners, send_ref, out_ref, ssem, rsem):
    me = lax.axis_index("ev")
    dp = lax.axis_index("dp")
    greet([(dp, lax.rem(me + o, owners)) for o in range(1, owners)])
    copies = exchange(owners, me, send_ref, out_ref, ssem, rsem)
    for c in copies:
        c.start()
    out_ref[me] = send_ref[me]
    for c in copies:
        c.wait()


def pick(rows, columns, of_row):
    hit = iota((rows, columns), 1) == of_row(iota((rows, columns), 0))
    return jnp.where(hit, 1.0, 0.0).astype(BF16)


def cross_section(owners, cap, layout, land_ref, gain_ref, win_ref, wout_ref, om_ref, bl_ref,
                  back_ref, grad_ref):
    me = lax.axis_index("ev")
    pieces, replicas, width = layout
    total = owners * cap
    d = land_ref.shape[-1]
    if cap % 16 == 0:
        rows = jnp.concatenate([land_ref[s, 0:cap] for s in range(owners)], axis=0)
        cot = jnp.concatenate([land_ref[s, cap : 2 * cap] for s in range(owners)], axis=0)
    else:
        landed = jnp.concatenate([land_ref[s] for s in range(owners)], axis=0)
        rows = dot(pick(total, 2 * total, lambda i: i + i // cap * cap), landed).astype(BF16)
        cot = dot(pick(total, 2 * total, lambda i: i + i // cap * cap + cap), landed).astype(BF16)
    gain = gain_ref[...]
    rows32 = rows.astype(F32)
    center, rstd = norm_stats(rows32)
    normed = (center * rstd * gain).astype(BF16)
    packed = dot(normed, win_ref[...]).astype(BF16)
    back_mixed = dot_bt(cot, wout_ref[...]).astype(BF16)

    table = owner_rows(om_ref, owners)
    count = jnp.sum(jnp.where(table == me, 1, 0), axis=1, keepdims=True)
    column = iota((owners, total), 1)
    of_source = jnp.where(column // cap == iota((owners, total), 0), count, 0)
    column_count = jnp.sum(of_source, axis=0, keepdims=True)
    live = (iota((1, total), 1) % cap) < column_count
    q_row, k_row = iota((total, total), 0), iota((total, total), 1)
    times = jnp.zeros((total, total), jnp.int32)
    blocks, listed = bl_ref.shape[2], bl_ref.shape[3]
    for b in range(blocks):
        named = jnp.where(k_row // BLOCK == b, 1, 0)
        for i in range(listed):
            named = named + jnp.where(k_row // BLOCK == bl_ref[0, 0, b, i], 1, 0)
        times = jnp.where(q_row // BLOCK == b, named, times)
    times = jnp.where(live, times, jnp.where(q_row == k_row, 1, 0)).astype(F32)
    times = jnp.concatenate([times, times], axis=0)
    kept = times > 0.0

    mixed, dq, dk, dv = [], [], [], []
    for t in range(d // BLOCK):
        q = packed[:, t * BLOCK : (t + 1) * BLOCK]
        k = packed[:, d + t * BLOCK : d + (t + 1) * BLOCK]
        v = packed[:, 2 * d + t * BLOCK : 2 * d + (t + 1) * BLOCK]
        q2 = two_heads(q)
        s = jnp.where(kept, dot_bt(q2, k) * SCALE, -1e30)
        w = jnp.where(kept, jnp.exp(s - jnp.max(s, axis=-1, keepdims=True)), 0.0)
        p = w / jnp.sum(w * times, axis=-1, keepdims=True)
        pm = (p.astype(BF16).astype(F32) * times).astype(BF16)
        mixed.append(join_heads(dot(pm, v)).astype(BF16))
        dm = two_heads(back_mixed[:, t * BLOCK : (t + 1) * BLOCK])
        dp = dot_bt(dm, v).astype(BF16).astype(F32)
        pt = p * times
        ds = (pt * (dp - jnp.sum(pt * dp, axis=-1, keepdims=True)) * SCALE).astype(BF16)
        dq.append(join_heads(dot(ds, k)).astype(BF16))
        dk.append(dot_at(ds, q2).astype(BF16))
        dv.append(dot_at(pm, dm).astype(BF16))
    mixed = jnp.concatenate(mixed, axis=1)
    back_packed = jnp.concatenate(dq + dk + dv, axis=1)
    result = dot(mixed, wout_ref[...]).astype(BF16)
    back_rows = norm_back(rows32, gain, dot_bt(back_packed, win_ref[...])).astype(BF16)
    if cap % 16 == 0:
        for s in range(owners):
            back_ref[s, 0:cap] = result[s * cap : (s + 1) * cap]
            back_ref[s, cap : 2 * cap] = back_rows[s * cap : (s + 1) * cap]
    else:
        both = jnp.concatenate([result, back_rows], axis=0)
        order = pick(
            2 * total, 2 * total,
            lambda i: i // (2 * cap) * cap + i % cap + (i % (2 * cap)) // cap * total,
        )
        both = dot(order, both).astype(BF16)
        for s in range(owners):
            back_ref[s] = both[s * 2 * cap : (s + 1) * 2 * cap]
    normed_t = normed.T
    mixed_t = mixed.T
    for k in range(pieces):
        for part in range(replicas):
            at = (k * replicas + part) * width
            if at < 3 * d:
                block = dot(normed_t, back_packed[:, at : at + width])
            else:
                block = dot(mixed_t, cot[:, at - 3 * d : at - 3 * d + width])
            half = replicas // 2
            grad_ref[k, part // half, part % half] = block.astype(BF16)


def closing(owners, cap, layout, factor, back_ref, grad_ref, x_ref, ct_ref, hid_ref, packed_ref, probs_ref,
            gain_ref, win_ref, wout_ref, om_ref,
            out_ref, gx_ref, gproj_ref, gout_ref,
            ret, ra, sa, rb, sb, rc, sc, gat,
            xs, xr, as_, ar, bs, br, cs, cr, ds_, dr):
    me = lax.axis_index("ev")
    dp = lax.axis_index("dp")
    pieces, replicas, width = layout
    xs_n = replicas // 2
    x_me, core = dp // 2, dp % 2
    d = x_ref.shape[-1]
    depth = d // owners

    greet([(dp, lax.rem(me + o, owners)) for o in range(1, owners)]
          + [(lax.rem(dp + o, replicas), me) for o in range(1, replicas)])

    def remote(src, dst, ss, rs, to):
        c = pltpu.make_async_remote_copy(
            src_ref=src, dst_ref=dst, send_sem=ss, recv_sem=rs, device_id=to, device_id_type=MESH)
        c.start()
        return c

    sent = []
    rows_back = exchange(owners, me, back_ref, ret, xs, xr)
    for c in rows_back:
        c.start()
    a = [remote(grad_ref.at[k, 1 - core], ra.at[k], as_.at[k], ar.at[k], (x_me * 2 + 1 - core, me))
         for k in range(pieces)]
    b, c_, d_ = {}, {}, {}

    def after_a(k):
        a[k].wait()
        for i in range(xs_n):
            sa[k, i] = (grad_ref[k, core, i].astype(F32) + ra[k, i].astype(F32)).astype(BF16)
        b[k] = []
        for o in range(1, xs_n):
            to = lax.rem(x_me + o, xs_n)
            b[k].append(remote(sa.at[k, to], rb.at[k, o - 1], bs.at[k, o - 1], br.at[k, o - 1],
                               (to * 2 + core, me)))

    def after_b(k):
        for c in b[k]:
            c.wait()
        total = sa[k, x_me].astype(F32)
        for o in range(1, xs_n):
            total = total + rb[k, o - 1].astype(F32)
        total = total.astype(BF16)
        for e in range(owners):
            sb[k, e] = total[e * depth : (e + 1) * depth]
        c_[k] = []
        for o in range(1, owners):
            to = lax.rem(me + o, owners)
            c_[k].append(remote(sb.at[k, to], rc.at[k, o - 1], cs.at[k, o - 1], cr.at[k, o - 1], (dp, to)))

    def after_c(k):
        for c in c_[k]:
            c.wait()
        total = sb[k, me].astype(F32)
        for o in range(1, owners):
            total = total + rc[k, o - 1].astype(F32)
        total = total.astype(BF16)
        sc[k] = total
        part = core * xs_n + x_me
        gat[k, part] = total
        d_[k] = []
        for o in range(1, replicas):
            to = lax.rem(dp + o, replicas)
            d_[k].append(remote(sc.at[k], gat.at[k, part], ds_.at[k, o - 1], dr.at[k, o - 1], (to, me)))

    def after_d(k):
        for c in d_[k]:
            c.wait()
        for part in range(replicas):
            at = (k * replicas + part) * width
            value = gat[k, part].astype(F32) * factor
            if at < 3 * d:
                gproj_ref[:, at : at + width] = value
            else:
                gout_ref[:, at - 3 * d : at - 3 * d + width] = value

    ret[me] = back_ref[me]
    place = placement(om_ref, owners, cap, me)
    for k in range(pieces):
        after_a(k)
    for c in rows_back:
        c.wait()
    returned = jnp.concatenate([ret[s] for s in range(owners)], axis=0)
    rows = dot_at(place, returned)
    out_ref[0] = (hid_ref[...].astype(F32) + rows[:BLOCK]).astype(BF16)
    grad_hidden = (ct_ref[0].astype(F32) + rows[BLOCK:]).astype(BF16)
    d_mixed = dot_bt(grad_hidden, wout_ref[...]).astype(BF16)
    dq, dk, dv = [], [], []
    pairs = d // BLOCK
    for t in range(pairs):
        q = packed_ref[:, t * BLOCK : (t + 1) * BLOCK]
        k = packed_ref[:, d + t * BLOCK : d + (t + 1) * BLOCK]
        v = packed_ref[:, 2 * d + t * BLOCK : 2 * d + (t + 1) * BLOCK]
        p = probs_ref[t]
        dm = two_heads(d_mixed[:, t * BLOCK : (t + 1) * BLOCK])
        d_p = dot_bt(dm, v).astype(BF16).astype(F32)
        ds = (p * (d_p - jnp.sum(p * d_p, axis=-1, keepdims=True)) * SCALE).astype(BF16)
        dq.append(join_heads(dot(ds, k)).astype(BF16))
        dk.append(dot_at(ds, two_heads(q)).astype(BF16))
        dv.append(dot_at(p.astype(BF16), dm).astype(BF16))
    after_b(0)
    d_packed = jnp.concatenate(dq + dk + dv, axis=1)
    d_normed = dot_bt(d_packed, win_ref[...]).astype(BF16).astype(F32)
    dx = norm_back(x_ref[0].astype(F32), gain_ref[...], d_normed).astype(BF16)
    gx_ref[0] = (grad_hidden.astype(F32) + dx.astype(F32)).astype(BF16)
    for k in range(1, pieces):
        after_b(k)
    for k in range(pieces):
        after_c(k)
    for k in range(pieces):
        after_d(k)


def call(body, outs, ins, scratch=(), collective=None, smem=()):
    vm = pl.BlockSpec(memory_space=pltpu.VMEM)
    sm = pl.BlockSpec(memory_space=pltpu.SMEM)
    extra = {} if collective is None else dict(collective_id=collective, has_side_effects=True)
    return pl.pallas_call(
        body,
        out_shape=[jax.ShapeDtypeStruct(s, t) for s, t in outs],
        in_specs=[sm if i in smem else vm for i in range(len(ins))],
        out_specs=[vm] * len(outs),
        scratch_shapes=list(scratch),
        compiler_params=pltpu.CompilerParams(vmem_limit_bytes=VMEM_LIMIT, **extra),
    )(*ins)


def on_device(events, cotangent, intra_gain, intra_proj, intra_out, cross_norm_gain,
              cross_input_weight, cross_output_weight, owner_map, block_lists):
    _, local_rows, d = events.shape
    owners = lax.axis_size("ev")
    replicas = lax.axis_size("dp")
    cap = 2 * local_rows // owners
    pieces = 2
    width = 4 * d // replicas // pieces
    layout = (pieces, replicas, width)
    depth = d // owners
    half = replicas // 2
    factor = (replicas * owners * local_rows) ** (-0.5)
    gain1 = intra_gain.reshape(1, d)
    gain2 = cross_norm_gain.reshape(1, d)
    dma = pltpu.SemaphoreType.DMA
    exchanged = ((owners, 2 * cap, d), BF16)

    hidden, outgoing, packed, probs = call(
        functools.partial(intra_forward, owners, cap),
        [((local_rows, d), BF16), exchanged, ((local_rows, 3 * d), BF16),
         ((d // BLOCK, 2 * BLOCK, BLOCK), F32)],
        [events, cotangent, gain1, intra_proj, intra_out, owner_map],
    )
    [landed] = call(
        functools.partial(exchange_kernel, owners), [exchanged], [outgoing],
        [dma((owners,)), dma((owners,))], collective=0,
    )
    back, grads = call(
        functools.partial(cross_section, owners, cap, layout),
        [exchanged, ((pieces, 2, half, d, width), BF16)],
        [landed, gain2, cross_input_weight, cross_output_weight, owner_map, block_lists],
        smem=(5,),
    )
    few = max(half - 1, 1)
    scratch = [
        pltpu.VMEM((owners, 2 * cap, d), BF16),
        pltpu.VMEM((pieces, half, d, width), BF16),
        pltpu.VMEM((pieces, half, d, width), BF16),
        pltpu.VMEM((pieces, few, d, width), BF16),
        pltpu.VMEM((pieces, owners, depth, width), BF16),
        pltpu.VMEM((pieces, owners - 1, depth, width), BF16),
        pltpu.VMEM((pieces, depth, width), BF16),
        pltpu.VMEM((pieces, replicas, depth, width), BF16),
        dma((owners,)), dma((owners,)),
        dma((pieces,)), dma((pieces,)),
        dma((pieces, few)), dma((pieces, few)),
        dma((pieces, owners - 1)), dma((pieces, owners - 1)),
        dma((pieces, replicas - 1)), dma((pieces, replicas - 1)),
    ]
    return tuple(call(
        functools.partial(closing, owners, cap, layout, factor),
        [((1, local_rows, d), BF16), ((1, local_rows, d), BF16),
         ((depth, 3 * d), F32), ((depth, d), F32)],
        [back, grads, events, cotangent, hidden, packed, probs, gain1, intra_proj, intra_out, owner_map],
        scratch, collective=1,
    ))


def solution(mesh):
    row = P("dp", "ev", None)
    return jax.shard_map(
        on_device,
        mesh=mesh,
        in_specs=(row, row, P(), P(), P(), P(), P(), P(), P("dp", None), P("dp", "ev", None, None)),
        out_specs=(row, row, P("ev", None), P("ev", None)),
        check_vma=False,
    )
```

time: 243 us -> 69 us (0.28)
  waiting for transfers between devices: 89.6 us -> 0 us
  Pallas kernels: 0 us -> 59.6 us
  local copies, waits for them, and re-layouts: 58.5 us -> 8.36 us
  matrix products: 31.7 us -> 0 us
  other arithmetic: 23.6 us -> 0 us
  starting transfers between devices: 23.3 us -> 0 us
  between operations: 15 us -> 0.73 us
    pallas_call x0 -> x4, Pallas kernels: none -> 59.6 us  [call(): pl.pallas_call(body, out_shape=[jax.ShapeDtypeStruct(s, t) for s, t in ou...]
    reduce_scatter x1 -> x0, waiting for transfers between devices: 42.2 us -> none  [on_device(): lax.psum_scatter(summed, 'ev', scatter_dimension=0, tiled=True)]
    psum x1 -> x0, waiting for transfers between devices: 32.6 us -> none  [on_device(): summed = lax.psum(partial_sum.astype(jnp.bfloat16), 'dp')]
    dot_general x22 -> x0, matrix products: 31.7 us -> none  [the longest x3 9.3 us: cross_account_inner(): jnp.einsum('bqhd,bkhd->bhqk', queries, key_rows) * HEAD_DIM ** (-0.5)]
    reshape x13 -> x0, local copies, waits for them, and re-layouts: 24.3 us -> none  [the longest x3 9.42 us: cross_account_inner(): key_rows = key_rows.reshape(block_groups, -1, HEADS, HEAD_DIM)]
    all_to_all x4 -> x0, starting transfers between devices: 23.2 us -> none  [the longest x1 7.28 us: on_device(): lax.all_to_all(outgoing, 'ev', split_axis=0, concat_axis=0, tiled=True)]
    all_to_all x4 -> x0, waiting for transfers between devices: 14.8 us -> none  [the longest x1 10.7 us: on_device(): lax.all_to_all(back_rows, 'ev', split_axis=0, concat_axis=0, tiled=True)]
    reduce_sum x13 -> x0, other arithmetic: 8.53 us -> none  [the longest x1 2.98 us: cross_account_inner(): weights = jnp.where(allowed, jnp.exp(scores - highest), 0.0)]
  transfers between devices with their start and end apart: 6 -> 0, of which waited for: 4 -> 0; matrix products, arithmetic and copies ran while one was open for 29% -> 0% of each run, Pallas kernels for 0% -> 0%
where the time goes in v1:
time: 69 us; the launch traced here: 68.7 us
  Pallas kernels  59.6 us (86%)
  local copies, waits for them, and re-layouts  8.36 us (12%)
  between operations  0.73 us (1%)
    pallas_call x4, Pallas kernels, call(): pl.pallas_call(body, out_shape=[jax.ShapeDtypeStruct(s, t) for s, t in ou...  59.6 us
    unnamed x28, local copies, waits for them, and re-layouts  8.36 us

profile of v1, /device:TPU:0, one launch (start us, length us, event | category | flops | bytes accessed | tf_op | source)
XLA Modules:
  0.0 68.7 jit_solution(1283860914998909679)
XLA Ops:
  0.6 0.0 copy-start
  0.6 1.4 %copy-done = bf16[512,1536]{1,0:T(8,128)(2,1)S(1)} copy-done((bf16[512,1536]{1,0:T(8,128)(2,1)S(1)}, bf16[512,1536]{1,0:T(8,128)(2,1)}, u32[]{:S(2)}) %copy-start) | copy-done | bytes 1572888
  2.0 0.0 copy-start.1
  2.0 1.0 %copy-done.1 = bf16[512,512]{1,0:T(8,128)(2,1)S(1)} copy-done((bf16[512,512]{1,0:T(8,128)(2,1)S(1)}, bf16[512,512]{1,0:T(8,128)(2,1)}, u32[]{:S(2)}) %copy-start.1) | copy-done | bytes 524312
  3.1 0.0 copy-start.5
  3.1 0.9 %copy-done.5 = bf16[1,128,512]{2,1,0:T(8,128)(2,1)S(1)} copy-done((bf16[1,128,512]{2,1,0:T(8,128)(2,1)S(1)}, bf16[1,128,512]{2,1,0:T(8,128)(2,1)}, u32[]{:S(2)}) %copy-start.5) | copy-done | bytes 131096
  4.0 0.0 copy-start.7
  4.0 0.9 %copy-done.7 = bf16[1,128,512]{2,1,0:T(8,128)(2,1)S(1)} copy-done((bf16[1,128,512]{2,1,0:T(8,128)(2,1)S(1)}, bf16[1,128,512]{2,1,0:T(8,128)(2,1)}, u32[]{:S(2)}) %copy-start.7) | copy-done | bytes 131096
  4.9 0.0 copy-start.8
  4.9 0.7 copy-done.8
  5.6 0.0 copy-start.9
  5.6 0.7 copy-done.9
  6.3 0.0 copy-start.3
  6.3 0.0 copy-start.4
  6.3 0.0 copy-start.10
  6.3 0.0 copy-start.11
  6.3 1.5 %shard_map.129 = (bf16[128,512]{1,0:T(8,128)(2,1)S(1)}, bf16[8,64,512]{2,1,0:T(8,128)(2,1)S(1)}, bf16[128,1536]{1,0:T(8,128)(2,1)S(1)}, f32[4,256,128]{2,1,0:T(8,128)S(1)}) custom-call(bf16[1,128,512]{2,1,0:T(8,128)(2,1)S(1)} %copy-done.5, bf16[1,128,512]{2,1,0:T(8,128)(2,1)S(1)} %copy-done.7, f32[1,512]{1,0:T(1,128)S(1)} %bitcast.2, ...), custom_call_target="tpu_custom_call" | custom-call | tf_op jit(solution)/shard_map/pallas_call | solution.py:363
  7.8 14.6 %shard_map.130.land_ref = bf16[8,64,512]{2,1,0:T(8,128)(2,1)S(1)} custom-call(bf16[8,64,512]{2,1,0:T(8,128)(2,1)S(1)} %get-tuple-element.10.send_ref), custom_call_target="tpu_custom_call" | custom-call | tf_op jit(solution)/shard_map/pallas_call | solution.py:363
  22.4 0.0 copy-done.3
  22.4 0.0 copy-done.4
  22.5 0.0 copy-done.10
  22.5 0.0 copy-done.11
  22.5 0.0 copy-start.2
  22.5 0.0 copy-start.6
  22.5 7.0 %shard_map.131 = (bf16[8,64,512]{2,1,0:T(8,128)(2,1)S(1)}, bf16[2,2,2,512,256]{4,3,2,1,0:T(8,128)(2,1)}) custom-call(bf16[8,64,512]{2,1,0:T(8,128)(2,1)S(1)} %shard_map.130.land_ref, f32[1,512]{1,0:T(1,128)S(1)} %bitcast.4, bf16[512,1536]{1,0:T(8,128)(2,1)S(1)} %copy-done.3, bf16[512,512]{1,0:T(8,128)(2,1)S(1)} %copy-done.4, s32[1,1024]{1,0:T(1,128)S(1)} %copy-done.8, ...), custom_call_target="tpu_custom_call" | custom-call | tf_op jit(solution)/shard_map/pallas_call | solution.py:363
  29.5 0.0 copy-done.2
  29.5 0.0 copy-done.6
  29.5 36.5 %shard_map.132 = (bf16[1,128,512]{2,1,0:T(8,128)(2,1)S(1)}, bf16[1,128,512]{2,1,0:T(8,128)(2,1)S(1)}, f32[64,1536]{1,0:T(8,128)S(1)}, f32[64,512]{1,0:T(8,128)S(1)}) custom-call(bf16[8,64,512]{2,1,0:T(8,128)(2,1)S(1)} %get-tuple-element.11.back_ref, bf16[2,2,2,512,256]{4,3,2,1,0:T(8,128)(2,1)} %get-tuple-element.12.grad_ref, ...), custom_call_target="tpu_custom_call" | custom-call | tf_op jit(solution)/shard_map/pallas_call | solution.py:363
  66.0 0.7 copy.18
  66.6 0.7 copy.19
  67.3 0.7 %copy.20 = f32[64,1536]{1,0:T(8,128)} copy(f32[64,1536]{1,0:T(8,128)S(1)} %get-tuple-element.22) | data formatting | bytes 786432
  68.0 0.7 copy.21
Async XLA Ops:
  0.6 1.4 %copy-start = (bf16[512,1536]{1,0:T(8,128)(2,1)S(1)}, bf16[512,1536]{1,0:T(8,128)(2,1)}, u32[]{:S(2)}) copy-start(bf16[512,1536]{1,0:T(8,128)(2,1)} %win_ref.5) | copy-start | bytes 4718596
  2.0 1.0 %copy-start.1 = (bf16[512,512]{1,0:T(8,128)(2,1)S(1)}, bf16[512,512]{1,0:T(8,128)(2,1)}, u32[]{:S(2)}) copy-start(bf16[512,512]{1,0:T(8,128)(2,1)} %wout_ref.5) | copy-start | bytes 1572868
  3.1 0.9 %copy-start.5 = (bf16[1,128,512]{2,1,0:T(8,128)(2,1)S(1)}, bf16[1,128,512]{2,1,0:T(8,128)(2,1)}, u32[]{:S(2)}) copy-start(bf16[1,128,512]{2,1,0:T(8,128)(2,1)} %x_ref.3) | copy-start | bytes 393220
  4.0 0.9 %copy-start.7 = (bf16[1,128,512]{2,1,0:T(8,128)(2,1)S(1)}, bf16[1,128,512]{2,1,0:T(8,128)(2,1)}, u32[]{:S(2)}) copy-start(bf16[1,128,512]{2,1,0:T(8,128)(2,1)} %ct_ref.3) | copy-start | bytes 393220
  4.9 0.7 copy-start.8
  5.6 0.7 copy-start.9
  6.3 16.2 %copy-start.3 = (bf16[512,1536]{1,0:T(8,128)(2,1)S(1)}, bf16[512,1536]{1,0:T(8,128)(2,1)}, u32[]{:S(2)}) copy-start(bf16[512,1536]{1,0:T(8,128)(2,1)} %win_ref.4) | copy-start | bytes 4718596
  6.3 16.2 %copy-start.4 = (bf16[512,512]{1,0:T(8,128)(2,1)S(1)}, bf16[512,512]{1,0:T(8,128)(2,1)}, u32[]{:S(2)}) copy-start(bf16[512,512]{1,0:T(8,128)(2,1)} %wout_ref.4) | copy-start | bytes 1572868
  6.3 16.2 %copy-start.10 = (f32[512]{0:T(512)S(1)}, f32[512]{0:T(512)}, u32[]{:S(2)}) copy-start(f32[512]{0:T(512)} %param.15) | copy-start | bytes 6148
  6.3 16.2 %copy-start.11 = (s32[1,1,2,2]{3,2,1,0:T(2,128)S(1)}, s32[1,1,2,2]{3,2,1,0:T(2,128)}, u32[]{:S(2)}) copy-start(s32[1,1,2,2]{3,2,1,0:T(2,128)} %bl_ref.1) | copy-start | bytes 52
  22.5 7.0 %copy-start.2 = (bf16[512,512]{1,0:T(8,128)(2,1)S(1)}, bf16[512,512]{1,0:T(8,128)(2,1)}, u32[]{:S(2)}) copy-start(bf16[512,512]{1,0:T(8,128)(2,1)} %wout_ref.5) | copy-start | bytes 1572868
  22.5 7.0 %copy-start.6 = (bf16[1,128,512]{2,1,0:T(8,128)(2,1)S(1)}, bf16[1,128,512]{2,1,0:T(8,128)(2,1)}, u32[]{:S(2)}) copy-start(bf16[1,128,512]{2,1,0:T(8,128)(2,1)} %x_ref.3) | copy-start | bytes 393220

commit v2 on v1

v2 whole, which is shorter than its diff:
```python
import functools

import jax
import jax.numpy as jnp
from jax import lax
from jax.experimental import pallas as pl
from jax.experimental.pallas import tpu as pltpu
from jax.sharding import PartitionSpec as P

HEAD_DIM = 64
BLOCK = 128
SCALE = HEAD_DIM ** (-0.5)
EPSILON = 1e-05
F32 = jnp.float32
BF16 = jnp.bfloat16
VMEM_LIMIT = 50 * 1024 * 1024
MESH = pl.DeviceIdType.MESH


def dot(a, b):
    return lax.dot_general(a, b, (((1,), (0,)), ((), ())), preferred_element_type=F32)


def dot_bt(a, b):
    return lax.dot_general(a, b, (((1,), (1,)), ((), ())), preferred_element_type=F32)


def dot_at(a, b):
    return lax.dot_general(a, b, (((0,), (0,)), ((), ())), preferred_element_type=F32)


def iota(shape, dim):
    return lax.broadcasted_iota(jnp.int32, shape, dim)


def norm_stats(x):
    center = x - jnp.mean(x, axis=-1, keepdims=True)
    rstd = lax.rsqrt(jnp.mean(center * center, axis=-1, keepdims=True) + EPSILON)
    return center, rstd


def norm_back(x, gain, dy):
    center, rstd = norm_stats(x)
    xhat = center * rstd
    g = dy * gain
    return rstd * (
        g
        - jnp.mean(g, axis=-1, keepdims=True)
        - xhat * jnp.mean(g * xhat, axis=-1, keepdims=True)
    )


def lane_masks(dtype):
    lane = iota((1, 2 * HEAD_DIM), 1)
    low = jnp.where(lane < HEAD_DIM, 1.0, 0.0).astype(F32)
    return low.astype(dtype), (1.0 - low).astype(dtype)


def two_heads(x):
    low, high = lane_masks(BF16)
    return jnp.concatenate([x * low, x * high], axis=0)


def join_heads(x):
    low, high = lane_masks(F32)
    half = x.shape[0] // 2
    return x[:half] * low + x[half:] * high


def owner_rows(owner_ref, owners):
    return jnp.concatenate(
        [owner_ref[:, s * BLOCK : (s + 1) * BLOCK] for s in range(owners)], axis=0
    )


def placement(owner_ref, owners, cap, me):
    table = owner_rows(owner_ref, owners)
    own = jnp.sum(jnp.where(iota(table.shape, 0) == me, table, 0), axis=0, keepdims=True)
    onehot = jnp.where(iota((owners, BLOCK), 0) == own, 1.0, 0.0).astype(F32)
    earlier = jnp.where(iota((BLOCK, BLOCK), 0) < iota((BLOCK, BLOCK), 1), 1.0, 0.0)
    before = dot(onehot.astype(BF16), earlier.astype(BF16))
    slot = jnp.sum(before * onehot, axis=0, keepdims=True).astype(jnp.int32)
    hit = iota((owners * cap, BLOCK), 0) == own * cap + slot
    return jnp.where(hit, 1.0, 0.0).astype(BF16)


def split_rows(ref, rows, owners, cap):
    for s in range(owners):
        ref[s] = rows[s * cap : (s + 1) * cap].astype(BF16)


def join_rows(ref, owners, cap):
    if cap % 16 == 0:
        return jnp.concatenate([ref[s] for s in range(owners)], axis=0)
    return jnp.concatenate([ref[s].astype(F32) for s in range(owners)], axis=0).astype(BF16)


def key_counts(om_ref, bl_ref, owners, cap, me):
    total = owners * cap
    table = owner_rows(om_ref, owners)
    count = jnp.sum(jnp.where(table == me, 1, 0), axis=1, keepdims=True)
    column = iota((owners, total), 1)
    of_source = jnp.where(column // cap == iota((owners, total), 0), count, 0)
    column_count = jnp.sum(of_source, axis=0, keepdims=True)
    live = (iota((1, total), 1) % cap) < column_count
    q_row, k_row = iota((total, total), 0), iota((total, total), 1)
    times = jnp.zeros((total, total), jnp.int32)
    blocks, listed = bl_ref.shape[2], bl_ref.shape[3]
    for b in range(blocks):
        named = jnp.where(k_row // BLOCK == b, 1, 0)
        for i in range(listed):
            named = named + jnp.where(k_row // BLOCK == bl_ref[0, 0, b, i], 1, 0)
        times = jnp.where(q_row // BLOCK == b, named, times)
    times = jnp.where(live, times, jnp.where(q_row == k_row, 1, 0)).astype(F32)
    return jnp.concatenate([times, times], axis=0)


def triple(packed, t, d):
    return tuple(packed[:, i * d + t * BLOCK : i * d + (t + 1) * BLOCK] for i in range(3))


def fused(owners, cap, layout, factor,
          x_hbm, ct_hbm, om_hbm, g1_hbm, win1_hbm, wout1_hbm, g2_hbm, win2_hbm, wout2_hbm, bl_ref,
          out_ref, gx_ref, gproj_ref, gout_ref,
          x_ref, ct_ref, om_ref, g1_ref, win1_ref, wout1_ref, g2_ref, win2_ref, wout2_ref,
          packed_ref, probs_ref, hid_ref, times_ref, p2_ref, grad_ref,
          cot_s, cot_r, hid_s, hid_r, res_s, res_r, bck_s, bck_r,
          ra, sa, rb, sb, ry, sy, rc, sc, gat,
          load_sem, row_ss, row_rs, as_, ar, bs, br, ys, yr, cs, cr, ds_, dr):
    me = lax.axis_index("ev")
    dp = lax.axis_index("dp")
    pieces, replicas, width = layout
    xs_n, zs_n = replicas // 2, owners // 2
    x_me, core = dp // 2, dp % 2
    z_me, y_me = me // 2, me % 2
    d = x_ref.shape[-1]
    depth = d // owners
    pairs = d // BLOCK

    loads = {}
    for i, (name, src, dst) in enumerate([
        ("om", om_hbm, om_ref), ("ct", ct_hbm, ct_ref), ("x", x_hbm, x_ref), ("g1", g1_hbm, g1_ref),
        ("win1", win1_hbm, win1_ref), ("wout1", wout1_hbm, wout1_ref), ("g2", g2_hbm, g2_ref),
        ("win2", win2_hbm, win2_ref), ("wout2", wout2_hbm, wout2_ref),
    ]):
        loads[name] = pltpu.make_async_copy(src, dst, load_sem.at[i])
        loads[name].start()

    peers = ([(dp, lax.rem(me + o, owners)) for o in range(1, owners)]
             + [(lax.rem(dp + o, replicas), me) for o in range(1, replicas)])
    barrier = pltpu.get_barrier_semaphore()
    for peer in peers:
        pl.semaphore_signal(barrier, inc=1, device_id=peer, device_id_type=MESH)

    loads["om"].wait()
    place = placement(om_ref, owners, cap, me)
    loads["ct"].wait()
    split_rows(cot_s, dot(place, ct_ref[0]), owners, cap)
    pl.semaphore_wait(barrier, len(peers))

    def remote(src, dst, ss, rs, to):
        c = pltpu.make_async_remote_copy(
            src_ref=src, dst_ref=dst, send_sem=ss, recv_sem=rs, device_id=to, device_id_type=MESH)
        c.start()
        return c

    def exchange(n, send, recv):
        copies = []
        for o in range(1, owners):
            to = lax.rem(me + o, owners)
            copies.append(remote(send.at[to], recv.at[me], row_ss.at[n, o], row_rs.at[n, o], (dp, to)))
        recv[me] = send[me]
        return copies

    def finish(copies):
        for c in copies:
            c.wait()

    cot_x = exchange(0, cot_s, cot_r)

    for name in ("x", "g1", "win1", "wout1"):
        loads[name].wait()
    x = x_ref[0].astype(F32)
    center, rstd = norm_stats(x)
    packed = dot((center * rstd * g1_ref[...]).astype(BF16), win1_ref[...]).astype(BF16)
    packed_ref[...] = packed
    mixed = []
    for t in range(pairs):
        q, k, v = triple(packed, t, d)
        s = dot_bt(two_heads(q), k) * SCALE
        w = jnp.exp(s - jnp.max(s, axis=-1, keepdims=True))
        p = w / jnp.sum(w, axis=-1, keepdims=True)
        probs_ref[t] = p
        mixed.append(join_heads(dot(p.astype(BF16), v)).astype(BF16))
    hidden = (x + dot(jnp.concatenate(mixed, axis=1), wout1_ref[...])).astype(BF16)
    hid_ref[...] = hidden
    split_rows(hid_s, dot(place, hidden), owners, cap)
    hid_x = exchange(1, hid_s, hid_r)

    times_ref[...] = key_counts(om_ref, bl_ref, owners, cap, me)
    for name in ("g2", "win2", "wout2"):
        loads[name].wait()
    gain = g2_ref[...]
    finish(hid_x)
    rows32 = join_rows(hid_r, owners, cap).astype(F32)
    center, rstd = norm_stats(rows32)
    normed = (center * rstd * gain).astype(BF16)
    packed = dot(normed, win2_ref[...]).astype(BF16)
    mixed = []
    for t in range(pairs):
        q, k, v = triple(packed, t, d)
        times = times_ref[...]
        s = jnp.where(times > 0.0, dot_bt(two_heads(q), k) * SCALE, -1e30)
        w = jnp.where(times > 0.0, jnp.exp(s - jnp.max(s, axis=-1, keepdims=True)), 0.0)
        p = w / jnp.sum(w * times, axis=-1, keepdims=True)
        p2_ref[t] = p
        pm = (p.astype(BF16).astype(F32) * times).astype(BF16)
        mixed.append(join_heads(dot(pm, v)).astype(BF16))
    mixed = jnp.concatenate(mixed, axis=1)
    split_rows(res_s, dot(mixed, wout2_ref[...]), owners, cap)
    res_x = exchange(2, res_s, res_r)

    a, b, y_, c_, d_ = {}, {}, {}, {}, {}

    def begin(k, left_t, right):
        block = dot(left_t, right).astype(BF16)
        for part in range(replicas):
            grad_ref[k, part // xs_n, part % xs_n] = block[:, part * width : (part + 1) * width]
        a[k] = remote(grad_ref.at[k, 1 - core], ra.at[k], as_.at[k], ar.at[k],
                      (x_me * 2 + 1 - core, me))

    def after_a(k):
        a[k].wait()
        for i in range(xs_n):
            sa[k, i] = (grad_ref[k, core, i].astype(F32) + ra[k, i].astype(F32)).astype(BF16)
        b[k] = []
        for o in range(1, xs_n):
            to = lax.rem(x_me + o, xs_n)
            b[k].append(remote(sa.at[k, to], rb.at[k, o - 1], bs.at[k, o - 1], br.at[k, o - 1],
                               (to * 2 + core, me)))

    def after_b(k):
        finish(b[k])
        total = sa[k, x_me].astype(F32)
        for o in range(1, xs_n):
            total = total + rb[k, o - 1].astype(F32)
        total = total.astype(BF16)
        for e in range(owners):
            sb[k, e % 2, e // 2] = total[e * depth : (e + 1) * depth]
        y_[k] = remote(sb.at[k, 1 - y_me], ry.at[k], ys.at[k], yr.at[k], (dp, z_me * 2 + 1 - y_me))

    def after_y(k):
        y_[k].wait()
        for z in range(zs_n):
            sy[k, z] = (sb[k, y_me, z].astype(F32) + ry[k, z].astype(F32)).astype(BF16)
        c_[k] = []
        for o in range(1, zs_n):
            to = lax.rem(z_me + o, zs_n)
            c_[k].append(remote(sy.at[k, to], rc.at[k, o - 1], cs.at[k, o - 1], cr.at[k, o - 1],
                                (dp, to * 2 + y_me)))

    def after_c(k):
        finish(c_[k])
        total = sy[k, z_me].astype(F32)
        for o in range(1, zs_n):
            total = total + rc[k, o - 1].astype(F32)
        total = total.astype(BF16)
        sc[k] = total
        part = core * xs_n + x_me
        gat[k, part] = total
        d_[k] = []
        for o in range(1, replicas):
            to = lax.rem(dp + o, replicas)
            d_[k].append(remote(sc.at[k], gat.at[k, part], ds_.at[k, o - 1], dr.at[k, o - 1], (to, me)))

    def after_d(k):
        finish(d_[k])
        for part in range(replicas):
            at = (k * replicas + part) * width
            value = gat[k, part].astype(F32) * factor
            if at < 3 * d:
                gproj_ref[:, at : at + width] = value
            else:
                gout_ref[:, at - 3 * d : at - 3 * d + width] = value

    finish(cot_x)
    cot = join_rows(cot_r, owners, cap)
    span = replicas * width
    mixed_t, normed_t = mixed.T, normed.T
    early = [k for k in range(pieces) if k * span >= 3 * d]
    for k in early:
        begin(k, mixed_t, cot[:, k * span - 3 * d : (k + 1) * span - 3 * d])
    back_mixed = dot_bt(cot, wout2_ref[...]).astype(BF16)
    dq, dk, dv = [], [], []
    for t in range(pairs):
        q, k, v = triple(packed, t, d)
        p, times = p2_ref[t], times_ref[...]
        pm = (p.astype(BF16).astype(F32) * times).astype(BF16)
        dm = two_heads(back_mixed[:, t * BLOCK : (t + 1) * BLOCK])
        d_p = dot_bt(dm, v).astype(BF16).astype(F32)
        pt = p * times
        ds = (pt * (d_p - jnp.sum(pt * d_p, axis=-1, keepdims=True)) * SCALE).astype(BF16)
        dq.append(join_heads(dot(ds, k)).astype(BF16))
        dk.append(dot_at(ds, two_heads(q)).astype(BF16))
        dv.append(dot_at(pm, dm).astype(BF16))
    back_packed = jnp.concatenate(dq + dk + dv, axis=1)
    for k in range(pieces):
        if k in early:
            continue
        if (k + 1) * span <= 3 * d:
            begin(k, normed_t, back_packed[:, k * span : (k + 1) * span])
        else:
            begin_split = jnp.concatenate(
                [dot(normed_t, back_packed[:, k * span :]),
                 dot(mixed_t, cot[:, : (k + 1) * span - 3 * d])], axis=1)
            block = begin_split.astype(BF16)
            for part in range(replicas):
                grad_ref[k, part // xs_n, part % xs_n] = block[:, part * width : (part + 1) * width]
            a[k] = remote(grad_ref.at[k, 1 - core], ra.at[k], as_.at[k], ar.at[k],
                          (x_me * 2 + 1 - core, me))
    order = early + [k for k in range(pieces) if k not in early]
    for k in early:
        after_a(k)
    split_rows(bck_s, norm_back(rows32, gain, dot_bt(back_packed, win2_ref[...])), owners, cap)
    bck_x = exchange(3, bck_s, bck_r)
    for k in order:
        if k not in early:
            after_a(k)

    steps = [after_b, after_y, after_c, after_d]
    waves = [
        (step, order[w - n]) for w in range(len(order) + len(steps) - 1)
        for n, step in reversed(list(enumerate(steps))) if 0 <= w - n < len(order)]
    for step, k in waves[:3]:
        step(k)

    finish(res_x)
    finish(bck_x)
    out_ref[0] = (hid_ref[...].astype(F32) + dot_at(place, join_rows(res_r, owners, cap))).astype(BF16)
    grad_hidden = (ct_ref[0].astype(F32) + dot_at(place, join_rows(bck_r, owners, cap))).astype(BF16)
    d_mixed = dot_bt(grad_hidden, wout1_ref[...]).astype(BF16)
    dq, dk, dv = [], [], []
    for t in range(pairs):
        q, k, v = triple(packed_ref, t, d)
        p = probs_ref[t]
        dm = two_heads(d_mixed[:, t * BLOCK : (t + 1) * BLOCK])
        d_p = dot_bt(dm, v).astype(BF16).astype(F32)
        ds = (p * (d_p - jnp.sum(p * d_p, axis=-1, keepdims=True)) * SCALE).astype(BF16)
        dq.append(join_heads(dot(ds, k)).astype(BF16))
        dk.append(dot_at(ds, two_heads(q)).astype(BF16))
        dv.append(dot_at(p.astype(BF16), dm).astype(BF16))
    d_packed = jnp.concatenate(dq + dk + dv, axis=1)
    d_normed = dot_bt(d_packed, win1_ref[...]).astype(BF16).astype(F32)
    dx = norm_back(x_ref[0].astype(F32), g1_ref[...], d_normed).astype(BF16)
    gx_ref[0] = (grad_hidden.astype(F32) + dx.astype(F32)).astype(BF16)

    for step, k in waves[3:]:
        step(k)


def on_device(events, cotangent, intra_gain, intra_proj, intra_out, cross_norm_gain,
              cross_input_weight, cross_output_weight, owner_map, block_lists):
    _, local_rows, d = events.shape
    owners = lax.axis_size("ev")
    replicas = lax.axis_size("dp")
    cap = 2 * local_rows // owners
    total = owners * cap
    pieces = min(4, 4 * d // replicas // 128)
    width = 4 * d // replicas // pieces
    depth = d // owners
    half, zs = replicas // 2, owners // 2
    few = max(half - 1, 1)
    factor = (replicas * owners * local_rows) ** (-0.5)
    gain1 = intra_gain.reshape(1, d)
    gain2 = cross_norm_gain.reshape(1, d)
    dma = pltpu.SemaphoreType.DMA
    ins = [events, cotangent, owner_map, gain1, intra_proj, intra_out,
           gain2, cross_input_weight, cross_output_weight, block_lists]
    scratch = [pltpu.VMEM(a.shape, a.dtype) for a in ins[:9]] + [
        pltpu.VMEM((local_rows, 3 * d), BF16),
        pltpu.VMEM((d // BLOCK, 2 * BLOCK, BLOCK), F32),
        pltpu.VMEM((local_rows, d), BF16),
        pltpu.VMEM((2 * total, total), F32),
        pltpu.VMEM((d // BLOCK, 2 * total, total), F32),
        pltpu.VMEM((pieces, 2, half, d, width), BF16),
    ] + [pltpu.VMEM((owners, cap, d), BF16)] * 8 + [
        pltpu.VMEM((pieces, half, d, width), BF16),
        pltpu.VMEM((pieces, half, d, width), BF16),
        pltpu.VMEM((pieces, few, d, width), BF16),
        pltpu.VMEM((pieces, 2, zs, depth, width), BF16),
        pltpu.VMEM((pieces, zs, depth, width), BF16),
        pltpu.VMEM((pieces, zs, depth, width), BF16),
        pltpu.VMEM((pieces, zs - 1, depth, width), BF16),
        pltpu.VMEM((pieces, depth, width), BF16),
        pltpu.VMEM((pieces, replicas, depth, width), BF16),
        dma((9,)), dma((4, owners)), dma((4, owners)),
        dma((pieces,)), dma((pieces,)),
        dma((pieces, few)), dma((pieces, few)),
        dma((pieces,)), dma((pieces,)),
        dma((pieces, zs - 1)), dma((pieces, zs - 1)),
        dma((pieces, replicas - 1)), dma((pieces, replicas - 1)),
    ]
    vm = pl.BlockSpec(memory_space=pltpu.VMEM)
    outs = [((1, local_rows, d), BF16), ((1, local_rows, d), BF16),
            ((depth, 3 * d), F32), ((depth, d), F32)]
    return tuple(pl.pallas_call(
        functools.partial(fused, owners, cap, (pieces, replicas, width), factor),
        out_shape=[jax.ShapeDtypeStruct(s, t) for s, t in outs],
        in_specs=[pl.BlockSpec(memory_space=pltpu.HBM)] * 9 + [pl.BlockSpec(memory_space=pltpu.SMEM)],
        out_specs=[vm] * 4,
        scratch_shapes=scratch,
        compiler_params=pltpu.CompilerParams(
            vmem_limit_bytes=VMEM_LIMIT, collective_id=0, has_side_effects=True),
    )(*ins))


def solution(mesh):
    row = P("dp", "ev", None)
    return jax.shard_map(
        on_device,
        mesh=mesh,
        in_specs=(row, row, P(), P(), P(), P(), P(), P(), P("dp", None), P("dp", "ev", None, None)),
        out_specs=(row, row, P("ev", None), P("ev", None)),
        check_vma=False,
    )
```

time: 69 us -> 65.8 us (0.954)
  Pallas kernels: 59.6 us -> 54 us
  local copies, waits for them, and re-layouts: 8.36 us -> 10.7 us
    pallas_call x4 -> x1, Pallas kernels: 59.6 us -> 54 us  [on_device(): pl.pallas_call(functools.partial(fused, owners, cap, (pieces, replicas, w...]
    unnamed x28 -> x22, local copies, waits for them, and re-layouts: 8.36 us -> 10.7 us
where the time goes in v2:
time: 65.8 us; the launch traced here: 65.4 us
  Pallas kernels  54 us (82%)
  local copies, waits for them, and re-layouts  10.7 us (16%)
  between operations  0.66 us (1%)
    pallas_call x1, Pallas kernels, on_device(): pl.pallas_call(functools.partial(fused, owners, cap, (pieces, replicas, w...  54 us
    unnamed x22, local copies, waits for them, and re-layouts  10.7 us

profile of v2, /device:TPU:0, one launch (start us, length us, event | category | flops | bytes accessed | tf_op | source)
XLA Modules:
  0.0 65.4 jit_solution(5419793027051451171)
XLA Ops:
  0.6 0.0 copy-start
  0.6 1.4 %copy-done = bf16[512,1536]{1,0:T(8,128)(2,1)S(1)} copy-done((bf16[512,1536]{1,0:T(8,128)(2,1)S(1)}, bf16[512,1536]{1,0:T(8,128)(2,1)}, u32[]{:S(2)}) %copy-start) | copy-done | bytes 1572888
  2.0 0.0 copy-start.1
  2.0 1.0 %copy-done.1 = bf16[512,512]{1,0:T(8,128)(2,1)S(1)} copy-done((bf16[512,512]{1,0:T(8,128)(2,1)S(1)}, bf16[512,512]{1,0:T(8,128)(2,1)}, u32[]{:S(2)}) %copy-start.1) | copy-done | bytes 524312
  3.1 0.0 copy-start.2
  3.1 1.0 %copy-done.2 = bf16[512,512]{1,0:T(8,128)(2,1)S(1)} copy-done((bf16[512,512]{1,0:T(8,128)(2,1)S(1)}, bf16[512,512]{1,0:T(8,128)(2,1)}, u32[]{:S(2)}) %copy-start.2) | copy-done | bytes 524312
  4.1 0.0 copy-start.3
  4.1 0.9 %copy-done.3 = bf16[1,128,512]{2,1,0:T(8,128)(2,1)S(1)} copy-done((bf16[1,128,512]{2,1,0:T(8,128)(2,1)S(1)}, bf16[1,128,512]{2,1,0:T(8,128)(2,1)}, u32[]{:S(2)}) %copy-start.3) | copy-done | bytes 131096
  5.0 0.0 copy-start.4
  5.0 0.9 %copy-done.4 = bf16[1,128,512]{2,1,0:T(8,128)(2,1)S(1)} copy-done((bf16[1,128,512]{2,1,0:T(8,128)(2,1)S(1)}, bf16[1,128,512]{2,1,0:T(8,128)(2,1)}, u32[]{:S(2)}) %copy-start.4) | copy-done | bytes 131096
  5.9 0.0 copy-start.5
  5.9 0.7 %copy-done.5 = s32[1,1024]{1,0:T(1,128)S(1)} copy-done((s32[1,1024]{1,0:T(1,128)S(1)}, s32[1,1024]{1,0:T(1,128)}, u32[]{:S(2)}) %copy-start.5) | copy-done | bytes 4120
  6.6 0.0 copy-start.6
  6.6 0.7 %copy-done.6 = f32[512]{0:T(512)S(1)} copy-done((f32[512]{0:T(512)S(1)}, f32[512]{0:T(512)}, u32[]{:S(2)}) %copy-start.6) | copy-done | bytes 2072
  7.3 0.0 copy-start.7
  7.3 0.7 %copy-done.7 = f32[512]{0:T(512)S(1)} copy-done((f32[512]{0:T(512)S(1)}, f32[512]{0:T(512)}, u32[]{:S(2)}) %copy-start.7) | copy-done | bytes 2072
  8.0 0.0 copy-start.8
  8.0 0.7 %copy-done.8 = s32[1,1,2,2]{3,2,1,0:T(2,128)S(1)} copy-done((s32[1,1,2,2]{3,2,1,0:T(2,128)S(1)}, s32[1,1,2,2]{3,2,1,0:T(2,128)}, u32[]{:S(2)}) %copy-start.8) | copy-done | bytes 40
  8.7 54.0 %shard_map.129 = (bf16[1,128,512]{2,1,0:T(8,128)(2,1)S(1)}, bf16[1,128,512]{2,1,0:T(8,128)(2,1)S(1)}, f32[64,1536]{1,0:T(8,128)S(1)}, f32[64,512]{1,0:T(8,128)S(1)}) custom-call(bf16[1,128,512]{2,1,0:T(8,128)(2,1)S(1)} %copy-done.3, bf16[1,128,512]{2,1,0:T(8,128)(2,1)S(1)} %copy-done.4, s32[1,1024]{1,0:T(1,128)S(1)} %copy-done.5, f32[1,512]{1,0:T(1,128)S(1)} %bitcast.2, ...), custom_call_target="tpu_custom_call" | custom-call | tf_op jit(solution)/shard_map/pallas_call | solution.py:406
  62.7 0.7 %copy.18 = bf16[1,128,512]{2,1,0:T(8,128)(2,1)} copy(bf16[1,128,512]{2,1,0:T(8,128)(2,1)S(1)} %get-tuple-element.8) | data formatting | bytes 262144
  63.4 0.7 %copy.19 = bf16[1,128,512]{2,1,0:T(8,128)(2,1)} copy(bf16[1,128,512]{2,1,0:T(8,128)(2,1)S(1)} %get-tuple-element.9) | data formatting | bytes 262144
  64.0 0.7 %copy.20 = f32[64,1536]{1,0:T(8,128)} copy(f32[64,1536]{1,0:T(8,128)S(1)} %get-tuple-element.10) | data formatting | bytes 786432
  64.8 0.7 %copy.21 = f32[64,512]{1,0:T(8,128)} copy(f32[64,512]{1,0:T(8,128)S(1)} %get-tuple-element.11) | data formatting | bytes 262144
Async XLA Ops:
  0.6 1.4 %copy-start = (bf16[512,1536]{1,0:T(8,128)(2,1)S(1)}, bf16[512,1536]{1,0:T(8,128)(2,1)}, u32[]{:S(2)}) copy-start(bf16[512,1536]{1,0:T(8,128)(2,1)} %win1_hbm.1) | copy-start | bytes 4718596
  2.0 1.0 %copy-start.1 = (bf16[512,512]{1,0:T(8,128)(2,1)S(1)}, bf16[512,512]{1,0:T(8,128)(2,1)}, u32[]{:S(2)}) copy-start(bf16[512,512]{1,0:T(8,128)(2,1)} %wout1_hbm.1) | copy-start | bytes 1572868
  3.1 1.0 %copy-start.2 = (bf16[512,512]{1,0:T(8,128)(2,1)S(1)}, bf16[512,512]{1,0:T(8,128)(2,1)}, u32[]{:S(2)}) copy-start(bf16[512,512]{1,0:T(8,128)(2,1)} %wout2_hbm.1) | copy-start | bytes 1572868
  4.1 0.9 %copy-start.3 = (bf16[1,128,512]{2,1,0:T(8,128)(2,1)S(1)}, bf16[1,128,512]{2,1,0:T(8,128)(2,1)}, u32[]{:S(2)}) copy-start(bf16[1,128,512]{2,1,0:T(8,128)(2,1)} %x_hbm.1) | copy-start | bytes 393220
  5.0 0.9 %copy-start.4 = (bf16[1,128,512]{2,1,0:T(8,128)(2,1)S(1)}, bf16[1,128,512]{2,1,0:T(8,128)(2,1)}, u32[]{:S(2)}) copy-start(bf16[1,128,512]{2,1,0:T(8,128)(2,1)} %ct_hbm.1) | copy-start | bytes 393220
  5.9 0.7 %copy-start.5 = (s32[1,1024]{1,0:T(1,128)S(1)}, s32[1,1024]{1,0:T(1,128)}, u32[]{:S(2)}) copy-start(s32[1,1024]{1,0:T(1,128)} %om_hbm.1) | copy-start | bytes 12292
  6.6 0.7 %copy-start.6 = (f32[512]{0:T(512)S(1)}, f32[512]{0:T(512)}, u32[]{:S(2)}) copy-start(f32[512]{0:T(512)} %param.12) | copy-start | bytes 6148
  7.3 0.7 %copy-start.7 = (f32[512]{0:T(512)S(1)}, f32[512]{0:T(512)}, u32[]{:S(2)}) copy-start(f32[512]{0:T(512)} %param.15) | copy-start | bytes 6148
  8.0 0.7 %copy-start.8 = (s32[1,1,2,2]{3,2,1,0:T(2,128)S(1)}, s32[1,1,2,2]{3,2,1,0:T(2,128)}, u32[]{:S(2)}) copy-start(s32[1,1,2,2]{3,2,1,0:T(2,128)} %bl_ref.1) | copy-start | bytes 52

commit v3 on v2

--- a/solution.py
+++ b/solution.py
@@ -13,7 +13,7 @@
 EPSILON = 1e-05
 F32 = jnp.float32
 BF16 = jnp.bfloat16
-VMEM_LIMIT = 50 * 1024 * 1024
+VMEM_LIMIT = 63 * 1024 * 1024
 MESH = pl.DeviceIdType.MESH
 
 

time: 65.8 us -> 61.9 us (0.941)
  local copies, waits for them, and re-layouts: 10.7 us -> 6.47 us
    unnamed x22 -> x4, local copies, waits for them, and re-layouts: 10.7 us -> 6.47 us
where the time goes in v3:
time: 61.9 us; the launch traced here: 61.7 us
  Pallas kernels  54.6 us (88%)
  local copies, waits for them, and re-layouts  6.47 us (10%)
  between operations  0.64 us (1%)
    pallas_call x1, Pallas kernels, on_device(): pl.pallas_call(functools.partial(fused, owners, cap, (pieces, replicas, w...  54.6 us
    unnamed x4, local copies, waits for them, and re-layouts  6.47 us

profile of v3, /device:TPU:0, one launch (start us, length us, event | category | flops | bytes accessed | tf_op | source)
XLA Modules:
  0.0 61.7 jit_solution(3584785445229561300)
XLA Ops:
  0.6 54.6 %shard_map.129 = (bf16[1,128,512]{2,1,0:T(8,128)(2,1)}, bf16[1,128,512]{2,1,0:T(8,128)(2,1)}, f32[64,1536]{1,0:T(8,128)}, f32[64,512]{1,0:T(8,128)}) custom-call(bf16[1,128,512]{2,1,0:T(8,128)(2,1)} %x_hbm.1, bf16[1,128,512]{2,1,0:T(8,128)(2,1)} %ct_hbm.1, s32[1,1024]{1,0:T(1,128)} %om_hbm.1, f32[1,512]{1,0:T(1,128)} %bitcast.2, bf16[512,1536]{1,0:T(8,128)(2,1)} %win1_hbm.1, ...), custom_call_target="tpu_custom_call" | custom-call | tf_op jit(solution)/shard_map/pallas_call | solution.py:406
  55.2 1.6 %copy.18 = bf16[1,128,512]{2,1,0:T(8,128)(2,1)} copy(bf16[1,128,512]{2,1,0:T(8,128)(2,1)} %get-tuple-element.8) | data formatting | bytes 262144
  56.8 1.6 %copy.19 = bf16[1,128,512]{2,1,0:T(8,128)(2,1)} copy(bf16[1,128,512]{2,1,0:T(8,128)(2,1)} %get-tuple-element.9) | data formatting | bytes 262144
  58.4 1.8 %copy.20 = f32[64,1536]{1,0:T(8,128)} copy(f32[64,1536]{1,0:T(8,128)} %get-tuple-element.10) | data formatting | bytes 786432
  60.1 1.6 %copy.21 = f32[64,512]{1,0:T(8,128)} copy(f32[64,512]{1,0:T(8,128)} %get-tuple-element.11) | data formatting | bytes 262144

commit v4 on v3

--- a/solution.py
+++ b/solution.py
@@ -331,7 +331,7 @@
     waves = [
         (step, order[w - n]) for w in range(len(order) + len(steps) - 1)
         for n, step in reversed(list(enumerate(steps))) if 0 <= w - n < len(order)]
-    for step, k in waves[:3]:
+    for step, k in waves[:6]:
         step(k)
 
     finish(res_x)
@@ -354,7 +354,7 @@
     dx = norm_back(x_ref[0].astype(F32), g1_ref[...], d_normed).astype(BF16)
     gx_ref[0] = (grad_hidden.astype(F32) + dx.astype(F32)).astype(BF16)
 
-    for step, k in waves[3:]:
+    for step, k in waves[6:]:
         step(k)
 
 

time: 61.9 us -> 61.4 us (level)
  no operation moved by 1% of the time
where the time goes in v4:
time: 61.4 us; the launch traced here: 61.2 us
  Pallas kernels  54.1 us (88%)
  local copies, waits for them, and re-layouts  6.47 us (11%)
  between operations  0.64 us (1%)
    pallas_call x1, Pallas kernels, on_device(): pl.pallas_call(functools.partial(fused, owners, cap, (pieces, replicas, w...  54.1 us
    unnamed x4, local copies, waits for them, and re-layouts  6.47 us

profile of v4, /device:TPU:0, one launch (start us, length us, event | category | flops | bytes accessed | tf_op | source)
XLA Modules:
  0.0 61.2 jit_solution(4903994020527052467)
XLA Ops:
  0.6 54.1 %shard_map.129 = (bf16[1,128,512]{2,1,0:T(8,128)(2,1)}, bf16[1,128,512]{2,1,0:T(8,128)(2,1)}, f32[64,1536]{1,0:T(8,128)}, f32[64,512]{1,0:T(8,128)}) custom-call(bf16[1,128,512]{2,1,0:T(8,128)(2,1)} %x_hbm.1, bf16[1,128,512]{2,1,0:T(8,128)(2,1)} %ct_hbm.1, s32[1,1024]{1,0:T(1,128)} %om_hbm.1, f32[1,512]{1,0:T(1,128)} %bitcast.2, bf16[512,1536]{1,0:T(8,128)(2,1)} %win1_hbm.1, ...), custom_call_target="tpu_custom_call" | custom-call | tf_op jit(solution)/shard_map/pallas_call | solution.py:406
  54.7 1.6 %copy.18 = bf16[1,128,512]{2,1,0:T(8,128)(2,1)} copy(bf16[1,128,512]{2,1,0:T(8,128)(2,1)} %get-tuple-element.8) | data formatting | bytes 262144
  56.3 1.6 %copy.19 = bf16[1,128,512]{2,1,0:T(8,128)(2,1)} copy(bf16[1,128,512]{2,1,0:T(8,128)(2,1)} %get-tuple-element.9) | data formatting | bytes 262144
  57.9 1.8 %copy.20 = f32[64,1536]{1,0:T(8,128)} copy(f32[64,1536]{1,0:T(8,128)} %get-tuple-element.10) | data formatting | bytes 786432
  59.6 1.6 %copy.21 = f32[64,512]{1,0:T(8,128)} copy(f32[64,512]{1,0:T(8,128)} %get-tuple-element.11) | data formatting | bytes 262144
